TPU v7x, 128 devices: a whole 4x4x4 slice. The times are simulated.
128 devices in a mesh: rows: 8 (over x, core), cols: 16 (over y, z).
Axes of the slice: x: 4, y: 4, z: 4, core: 2. Of those that a mesh axis runs over, the one named last changes fastest.
Arguments:
- luminance: float32 [2048, 8192], P('rows', 'cols'), may hold values from 0 to 1
- grad_x: float32 [4, 2048, 8192], P(None, 'rows', 'cols'), may hold values from -0.6 to 0.6
- grad_y: float32 [4, 2048, 8192], P(None, 'rows', 'cols'), may hold values from -0.6 to 0.6
- labels: int32 [2048, 8192], P('rows', 'cols'), may hold values from 0 to 3
Outputs:
- stitched: float32 [2048, 8192], P('rows', 'cols')
All inputs are finite; a program needn't handle non-finite values.
Results may differ from a plain program's by a relative error of at most 0.0003.
Values sent between devices are 32-bit elements; how exact they have to be, the bound alone decides.
A program may use at most 128 MiB of HBM per device.

v0:
```python
import math

import jax
import jax.numpy as jnp
from jax import lax
from jax.sharding import PartitionSpec as P

NU = 2


screen_weight = 4e-06
omega = 0.8


def with_halo(x, sides, width):
    for axis, dim in sides:
        count, length = (lax.axis_size(axis), x.shape[dim])
        up = [(i, (i + 1) % count) for i in range(count - 1)]
        down = [(j, i) for i, j in up]
        last = lax.slice_in_dim(x, length - width, length, axis=dim)
        first = lax.slice_in_dim(x, 0, width, axis=dim)
        before = lax.ppermute(last, axis, up)
        after = lax.ppermute(first, axis, down)
        x = jnp.concatenate([before, x, after], axis=dim)
    return x


def passed_along(value, axis, steps):
    count = lax.axis_size(axis)
    first, last = (max(0, -steps), min(count, count - steps))
    return lax.ppermute(value, axis, [(source, source + steps) for source in range(first, last)])


def grid_frame(rows_local, cols_local, margin):
    total_rows = rows_local * lax.axis_size("rows")
    total_cols = cols_local * lax.axis_size("cols")
    row_ids = (
        lax.axis_index("rows") * rows_local
        - margin
        + jnp.arange(rows_local + 2 * margin, dtype=jnp.int32)
    )
    col_ids = (
        lax.axis_index("cols") * cols_local
        - margin
        + jnp.arange(cols_local + 2 * margin, dtype=jnp.int32)
    )
    row_part = (row_ids > 0).astype(jnp.float32) + (row_ids < total_rows - 1).astype(jnp.float32)
    col_part = (col_ids > 0).astype(jnp.float32) + (col_ids < total_cols - 1).astype(jnp.float32)
    deg = row_part[:, None] + col_part[None, :]
    row_in = ((row_ids >= 0) & (row_ids < total_rows)).astype(jnp.float32)
    col_in = ((col_ids >= 0) & (col_ids < total_cols)).astype(jnp.float32)
    return (deg, row_in[:, None] * col_in[None, :])


def neighbours(padded):
    return padded[2:, 1:-1] + padded[:-2, 1:-1] + padded[1:-1, 2:] + padded[1:-1, :-2]


def apply_local(field, deg, coef):
    padded = with_halo(field, (("rows", 0), ("cols", 1)), 1)
    return screen_weight * field + coef * (deg * field - neighbours(padded))


def smooth(field, rhs, coef):
    nrows, ncols = field.shape
    deg, inside = grid_frame(nrows, ncols, 0)
    diag = screen_weight + coef * deg
    for sweep in range(NU):
        field = field + omega * (rhs - apply_local(field, deg, coef)) / diag
    return field


def residual_of(field, rhs, coef):
    nrows, ncols = field.shape
    deg, inside = grid_frame(nrows, ncols, 0)
    return rhs - apply_local(field, deg, coef)


def restrict(field):
    nrows, ncols = field.shape
    return field.reshape(nrows // 2, 2, ncols // 2, 2).sum(axis=(1, 3)) * 0.25


def prolong(field):
    return jnp.repeat(jnp.repeat(field, 2, axis=0), 2, axis=1)


def table_at(count, freq_ids, place_ids):
    freq = freq_ids[:, None]
    place = place_ids[None, :]
    phase = (2 * place + 1) * freq % (4 * count)
    angle = phase.astype(jnp.float32) * (math.pi / (2 * count))
    scale = jnp.where(freq == 0, math.sqrt(1.0 / count), math.sqrt(2.0 / count))
    return scale * jnp.cos(angle)


def dct_table(count):
    ids = jnp.arange(count, dtype=jnp.int32)
    return table_at(count, ids, ids)


def eigen_part(width, count):
    freq = jnp.arange(width, dtype=jnp.int32).astype(jnp.float32)
    sine = jnp.sin(freq * (math.pi / (2 * count)))
    return 4.0 * sine * sine


def gathered_solve(coarse_two):
    band_rows, band_cols = coarse_two.shape
    hp = lax.Precision.HIGHEST
    band = lax.all_gather(coarse_two, "cols", axis=1, tiled=True)
    ccols = band.shape[1]
    crows = band_rows * lax.axis_size("rows")
    row_table = dct_table(crows)
    col_table = dct_table(ccols)
    col_start = lax.axis_index("cols") * band_cols
    whole = lax.all_gather(band, "rows", axis=0, tiled=True)
    lam = screen_weight + 0.25 * (
        eigen_part(crows, crows)[:, None] + eigen_part(ccols, ccols)[None, :]
    )
    modes = jnp.dot(jnp.dot(row_table, whole, precision=hp), col_table.T, precision=hp)
    solved = jnp.dot(jnp.dot(row_table.T, modes / lam, precision=hp), col_table, precision=hp)
    row_start = lax.axis_index("rows") * band_rows
    solved = lax.dynamic_slice_in_dim(solved, row_start, band_rows, 0)
    return lax.dynamic_slice_in_dim(solved, col_start, band_cols, 1)


def coarse_solve(coarse_two):
    return gathered_solve(coarse_two)


def shards(luminance, grad_x, grad_y, labels):
    nrows, ncols = luminance.shape
    lens_ids = jnp.arange(grad_x.shape[0], dtype=jnp.int32)[:, None, None]
    chosen = labels[None] == lens_ids
    sel_x = jnp.sum(jnp.where(chosen, grad_x, 0.0), axis=0)
    sel_y = jnp.sum(jnp.where(chosen, grad_y, 0.0), axis=0)
    total_rows = nrows * lax.axis_size("rows")
    total_cols = ncols * lax.axis_size("cols")
    col_ids = lax.axis_index("cols") * ncols + jnp.arange(ncols, dtype=jnp.int32)
    row_ids = lax.axis_index("rows") * nrows + jnp.arange(nrows, dtype=jnp.int32)
    sel_x = jnp.where(col_ids[None, :] < total_cols - 1, sel_x, 0.0)
    sel_y = jnp.where(row_ids[:, None] < total_rows - 1, sel_y, 0.0)
    left_edge = passed_along(sel_x[:, ncols - 1 :], "cols", 1)
    upper_edge = passed_along(sel_y[nrows - 1 :, :], "rows", 1)
    from_left = jnp.concatenate([left_edge, sel_x[:, : ncols - 1]], axis=1)
    from_up = jnp.concatenate([upper_edge, sel_y[: nrows - 1, :]], axis=0)
    rhs = screen_weight * luminance + from_left - sel_x + from_up - sel_y
    field = smooth(luminance, rhs, 1.0)
    coarse_one = restrict(residual_of(field, rhs, 1.0))
    err_one = smooth(jnp.zeros_like(coarse_one), coarse_one, 0.5)
    coarse_two = restrict(residual_of(err_one, coarse_one, 0.5))
    err_two = coarse_solve(coarse_two)
    err_one = smooth(err_one + prolong(err_two), coarse_one, 0.5)
    return smooth(field + prolong(err_one), rhs, 1.0)


def solution(mesh):
    return jax.shard_map(
        shards,
        mesh=mesh,
        in_specs=(
            P("rows", "cols"),
            P(None, "rows", "cols"),
            P(None, "rows", "cols"),
            P("rows", "cols"),
        ),
        out_specs=P("rows", "cols"),
        check_vma=False,
    )
```

profile of v0, /device:TPU:12, one launch (start us, length us, event | category | flops | bytes accessed | tf_op | source)
XLA Modules:
  0.0 502.7 jit_solution(11736457096456884999)
XLA Ops:
  6.5 3.1 select_reduce_fusion.1
  9.8 3.8 collective-permute-start
  13.8 1.9 collective-permute-start.1
  16.5 3.6 collective-permute-start.2
  20.1 1.9 collective-permute-start.3
  22.6 3.6 collective-permute-start.14
  27.4 4.1 collective-permute-start.4
  31.5 1.9 collective-permute-start.5
  33.5 1.9 collective-permute-start.15
  35.5 5.1 %collective-permute-done.5 = f32[258,1]{1,0:T(8,128)S(1)} collective-permute-done((f32[258,1]{1,0:T(8,128)S(1)}, f32[258,1]{1,0:T(8,128)S(1)}, u32[]{:S(2)}, u32[]{:S(2)}) %collective-permute-start.5) | collective-permute-done | bytes 1064 | tf_op jit(solution)/shard_map/ppermute | solution.py:22
  40.6 2.8 fusion.33
  43.4 1.9 collective-permute-start.6
  45.4 2.4 collective-permute-start.7
  47.8 2.5 collective-permute-done.7
  50.4 3.2 collective-permute-start.8
  53.6 2.6 collective-permute-start.9
  57.3 5.3 %collective-permute-done.9 = f32[258,1]{1,0:T(8,128)S(1)} collective-permute-done((f32[258,1]{1,0:T(8,128)S(1)}, f32[258,1]{1,0:T(8,128)S(1)}, u32[]{:S(2)}, u32[]{:S(2)}) %collective-permute-start.9) | collective-permute-done | bytes 1064 | tf_op jit(solution)/shard_map/ppermute | solution.py:22
  63.2 1.9 collective-permute-start.10
  65.1 2.4 collective-permute-start.11
  70.1 1.9 collective-permute-start.12
  72.1 3.9 collective-permute-start.13
  76.1 4.0 collective-permute-start.16
  80.1 1.9 collective-permute-start.17
  82.5 34.8 %reshape.105 = f32[128,2,256,2]{3,2,1,0:T(8,128)} reshape(f32[256,512]{1,0:T(8,128)S(1)} %fusion.47) | data formatting | bytes 1048576 | tf_op jit(solution)/shard_map/reshape | solution.py:81
  117.3 13.2 %reduce_sum.38 = f32[128,256]{1,0:T(8,128)S(1)} reduce(f32[128,2,256,2]{3,2,1,0:T(8,128)} %reshape.105, f32[]{:T(128)} %constant.34.clone.1), dimensions={1,3}, to_apply=%region_2.3 | reduce | flops 98304 | bytes 655364 | tf_op jit(solution)/shard_map/reduce_sum | solution.py:81
  131.5 1.9 collective-permute-start.18
  133.4 2.4 collective-permute-start.19
  135.9 2.5 collective-permute-done.19
  138.4 6.0 %collective-permute-start.20 = (f32[130,1]{1,0:T(8,128)S(1)}, f32[130,1]{1,0:T(8,128)S(1)}, u32[]{:S(2)}, u32[]{:S(2)}) collective-permute-start(f32[130,1]{1,0:T(8,128)S(1)} %get-tuple-element.35), channel_id=1, source_target_pairs={{1,0},{2,1},{3,2},{4,3},{5,4},{6,5},{7,6},{8,7},{9,8},{10,9},{11,1... | collective-permute-start | bytes 1568 | tf_op jit(solution)/shard_map/ppermute | solution.py:23
  144.5 1.9 collective-permute-start.21
  146.4 6.4 %collective-permute-done.21 = f32[130,1]{1,0:T(8,128)S(1)} collective-permute-done((f32[130,1]{1,0:T(8,128)S(1)}, f32[130,1]{1,0:T(8,128)S(1)}, u32[]{:S(2)}, u32[]{:S(2)}) %collective-permute-start.21) | collective-permute-done | bytes 552 | tf_op jit(solution)/shard_map/ppermute | solution.py:22
  153.0 1.9 collective-permute-start.22
  154.9 2.4 collective-permute-start.23
  157.3 2.5 collective-permute-done.23
  161.8 3.9 collective-permute-start.25
  166.1 4.0 collective-permute-done.25
  170.3 9.8 %reshape.106 = f32[64,2,128,2]{3,2,1,0:T(8,128)} reshape(f32[128,256]{1,0:T(8,128)S(1)} %fusion.100) | data formatting | bytes 262144 | tf_op jit(solution)/shard_map/reshape | solution.py:81
  180.1 4.5 reduce_sum.39
  184.7 25.2 %all_gather.6 = f32[64,2048]{1,0:T(8,128)} all-gather(f32[64,128]{1,0:T(8,128)S(1)} %broadcast_multiply_fusion), channel_id=1, replica_groups=mesh['rows'=8,'cols'=16] {'cols'}, dimensions={1}, use_global_device_ids=true | all-gather | bytes 557056 | tf_op jit(solution)/shard_map/all_gather | solution.py:111
  210.0 62.5 %fusion.175 = f32[2048,2048]{1,0:T(8,128)} fusion(s32[2048]{0:T(1024)S(1)} %multiply_add_fusion, f32[2048]{0:T(1024)S(1)} %fusion.123), kind=kLoop, calls=%fused_computation.7.clone.1.clone.1 | loop fusion | flops 62914560 | bytes 16793600 | tf_op jit(solution)/shard_map/dot_general | solution.py:121
  272.5 62.8 %fusion.173 = f32[2048,2048]{1,0:T(8,128)} fusion(s32[2048]{0:T(1024)S(1)} %multiply_add_fusion, f32[2048]{0:T(1024)S(1)} %fusion.123), kind=kLoop, calls=%fused_computation.7.clone.clone.1 | loop fusion | flops 62914560 | bytes 16793600 | tf_op jit(solution)/shard_map/dot_general | solution.py:122
  335.3 13.0 %fusion.75 = f32[512,2048]{1,0:T(8,128)S(1)} fusion(f32[512,2048]{1,0:T(8,128)} %all-gather.2.cloned.1.call-done, s32[512]{0:T(512)S(1)} %multiply_add_fusion.1, f32[512]{0:T(512)S(1)} %fusion.126), kind=kOutput, calls=%fused_computation.128 | convolution fusion | flops 6446383104 | bytes 8392704 | tf_op jit(solution)/shard_map/dot_general | solution.py:121
  348.4 30.6 %fusion.10 = f32[512,2048]{1,0:T(8,128)S(1)} fusion(f32[512,2048]{1,0:T(8,128)S(1)} %fusion.75, f32[2048,2048]{1,0:T(8,128)} %fusion.175), kind=kOutput, calls=%fused_computation.12 | convolution fusion | flops 25769803776 | bytes 25165824 | tf_op jit(solution)/shard_map/dot_general | solution.py:121
  378.9 11.9 %fusion.12 = f32[512,2048]{1,0:T(8,128)S(1)} fusion(f32[512,2048]{1,0:T(8,128)S(1)} %fusion.10, f32[2048]{0:T(1024)S(1)} %multiply_multiply_fusion, f32[512]{0:T(512)S(1)} %multiply_multiply_fusion.1, s32[512]{0:T(512)S(1)} %multiply_add_fusion.1, f32[512]{0:T(512)S(1)} %fusion.126), kind=kOutput, calls=%fused_computation.13 | convolution fusion | flops 6450577408 | bytes 8402944 | tf_op jit(solution)/shard_map/dot_general | solution.py:122
  390.9 27.7 %fusion.8 = f32[512,2048]{1,0:T(8,128)S(1)} fusion(f32[512,2048]{1,0:T(8,128)S(1)} %fusion.12, f32[2048,2048]{1,0:T(8,128)S(1)} %bitcast.14), kind=kOutput, calls=%fused_computation.11 | convolution fusion | flops 25769803776 | bytes 25165824 | tf_op jit(solution)/shard_map/dot_general | solution.py:122
  421.0 2.4 collective-permute-start.27
  423.4 2.5 collective-permute-done.27
  425.9 4.6 collective-permute-start.28
  432.5 6.4 %collective-permute-done.29 = f32[130,1]{1,0:T(8,128)S(1)} collective-permute-done((f32[130,1]{1,0:T(8,128)S(1)}, f32[130,1]{1,0:T(8,128)S(1)}, u32[]{:S(2)}, u32[]{:S(2)}) %collective-permute-start.29) | collective-permute-done | bytes 552 | tf_op jit(solution)/shard_map/ppermute | solution.py:22
  439.1 1.9 collective-permute-start.30
  441.0 2.4 collective-permute-start.31
  443.4 2.5 collective-permute-done.31
  447.9 3.9 collective-permute-start.33
  452.2 4.0 collective-permute-done.33
  459.6 2.4 collective-permute-start.35
  462.1 2.5 collective-permute-done.35
  466.6 3.9 collective-permute-start.37
  471.6 4.0 collective-permute-done.37
  476.2 1.9 collective-permute-start.38
  478.1 2.4 collective-permute-start.39
  480.5 2.5 collective-permute-done.39
  483.1 1.9 collective-permute-start.40
  485.1 3.9 collective-permute-start.41
  490.0 4.0 collective-permute-done.41
  (120 shorter events, 27.7 us)
Async XLA Ops:
  6.5 328.7 %all-gather.2.cloned.1.call-start = ((), (), s32[]{:S(2)}) async-start(), calls=%async_computation | async-start | bytes 4718592 | tf_op jit(solution)/shard_map/all_gather | solution.py:117
  6.5 3.2 copy-start.3
  9.8 23.7 %collective-permute-start = (f32[256,1]{1,0:T(8,128)S(1)}, f32[256,1]{1,0:T(8,128)S(1)}, u32[]{:S(2)}, u32[]{:S(2)}) collective-permute-start(f32[256,1]{1,0:T(8,128)S(1)} %slice.368), channel_id=1, source_target_pairs={{0,1},{1,2},{2,3},{3,4},{4,5},{5,6},{6,7},{7,8},{8,9},{9,10},{10,1... | collective-permute-start | bytes 3080 | tf_op jit(solution)/shard_map/ppermute | solution.py:31
  13.7 2.8 copy-start.4
  13.8 21.6 %collective-permute-start.1 = (f32[1,512]{1,0:T(1,128)S(1)}, f32[1,512]{1,0:T(1,128)S(1)}, u32[]{:S(2)}, u32[]{:S(2)}) collective-permute-start(f32[1,512]{1,0:T(1,128)S(1)} %slice.370), channel_id=1, source_target_pairs={{0,16},{16,32},{32,48},{48,64},{64,80},{80,96},{96,112},{1,17},{17... | collective-permute-start | bytes 6152 | tf_op jit(solution)/shard_map/ppermute | solution.py:31
  16.5 9.8 %collective-permute-start.2 = (f32[1,512]{1,0:T(1,128)S(1)}, f32[1,512]{1,0:T(1,128)S(1)}, u32[]{:S(2)}, u32[]{:S(2)}) collective-permute-start(f32[1,512]{1,0:T(1,128)S(1)} %get-tuple-element.28), channel_id=1, source_target_pairs={{16,0},{32,16},{48,32},{64,48},{80,64},{96,80},{112,96},{17,1},{33... | collective-permute-start | bytes 6152 | tf_op jit(solution)/shard_map/ppermute | solution.py:23
  20.1 6.2 %collective-permute-start.3 = (f32[1,512]{1,0:T(1,128)S(1)}, f32[1,512]{1,0:T(1,128)S(1)}, u32[]{:S(2)}, u32[]{:S(2)}) collective-permute-start(f32[1,512]{1,0:T(1,128)S(1)} %get-tuple-element.27), channel_id=1, source_target_pairs={{0,16},{16,32},{32,48},{48,64},{64,80},{80,96},{96,112},{1,17},{17... | collective-permute-start | bytes 6152 | tf_op jit(solution)/shard_map/ppermute | solution.py:22
  22.6 44.9 %collective-permute-start.14 = (f32[1,256]{1,0:T(1,128)}, f32[1,256]{1,0:T(1,128)}, u32[]{:S(2)}, u32[]{:S(2)}) collective-permute-start(f32[1,256]{1,0:T(1,128)} %broadcast.187), channel_id=1, source_target_pairs={{16,0},{32,16},{48,32},{64,48},{80,64},{96,80},{112,96},{17,1},{33... | collective-permute-start | bytes 3080 | tf_op jit(solution)/shard_map/ppermute | solution.py:23
  26.3 14.3 %copy-start = (f32[1,512]{1,0:T(1,128)}, f32[1,512]{1,0:T(1,128)S(1)}, u32[]{:S(2)}) copy-start(f32[1,512]{1,0:T(1,128)S(1)} %collective-permute-done.2) | copy-start | bytes 6148
  26.3 14.2 %copy-start.1 = (f32[1,512]{1,0:T(1,128)}, f32[1,512]{1,0:T(1,128)S(1)}, u32[]{:S(2)}) copy-start(f32[1,512]{1,0:T(1,128)S(1)} %collective-permute-done.3) | copy-start | bytes 6148
  27.4 8.0 %collective-permute-start.4 = (f32[258,1]{1,0:T(8,128)S(1)}, f32[258,1]{1,0:T(8,128)S(1)}, u32[]{:S(2)}, u32[]{:S(2)}) collective-permute-start(f32[258,1]{1,0:T(8,128)S(1)} %get-tuple-element.17), channel_id=1, source_target_pairs={{1,0},{2,1},{3,2},{4,3},{5,4},{6,5},{7,6},{8,7},{9,8},{10,9},{11,1... | collective-permute-start | bytes 3104 | tf_op jit(solution)/shard_map/ppermute | solution.py:23
  31.5 9.0 %collective-permute-start.5 = (f32[258,1]{1,0:T(8,128)S(1)}, f32[258,1]{1,0:T(8,128)S(1)}, u32[]{:S(2)}, u32[]{:S(2)}) collective-permute-start(f32[258,1]{1,0:T(8,128)S(1)} %get-tuple-element.18), channel_id=1, source_target_pairs={{0,1},{1,2},{2,3},{3,4},{4,5},{5,6},{6,7},{7,8},{8,9},{9,10},{10,1... | collective-permute-start | bytes 3104 | tf_op jit(solution)/shard_map/ppermute | solution.py:22
  33.5 34.0 %collective-permute-start.15 = (f32[1,256]{1,0:T(1,128)}, f32[1,256]{1,0:T(1,128)}, u32[]{:S(2)}, u32[]{:S(2)}) collective-permute-start(f32[1,256]{1,0:T(1,128)} %broadcast.187), channel_id=1, source_target_pairs={{0,16},{16,32},{32,48},{48,64},{64,80},{80,96},{96,112},{1,17},{17... | collective-permute-start | bytes 3080 | tf_op jit(solution)/shard_map/ppermute | solution.py:22
  35.4 5.1 %copy-start.2 = (f32[1,512]{1,0:T(1,128)}, f32[1,512]{1,0:T(1,128)S(1)}, u32[]{:S(2)}) copy-start(f32[1,512]{1,0:T(1,128)S(1)} %collective-permute-done.1) | copy-start | bytes 6148
  43.4 4.4 collective-permute-start.6
  45.4 4.9 collective-permute-start.7
  50.4 6.9 %collective-permute-start.8 = (f32[258,1]{1,0:T(8,128)S(1)}, f32[258,1]{1,0:T(8,128)S(1)}, u32[]{:S(2)}, u32[]{:S(2)}) collective-permute-start(f32[258,1]{1,0:T(8,128)S(1)} %get-tuple-element.15), channel_id=1, source_target_pairs={{1,0},{2,1},{3,2},{4,3},{5,4},{6,5},{7,6},{8,7},{9,8},{10,9},{11,1... | collective-permute-start | bytes 3104 | tf_op jit(solution)/shard_map/ppermute | solution.py:23
  53.6 9.0 %collective-permute-start.9 = (f32[258,1]{1,0:T(8,128)S(1)}, f32[258,1]{1,0:T(8,128)S(1)}, u32[]{:S(2)}, u32[]{:S(2)}) collective-permute-start(f32[258,1]{1,0:T(8,128)S(1)} %get-tuple-element.16), channel_id=1, source_target_pairs={{0,1},{1,2},{2,3},{3,4},{4,5},{5,6},{6,7},{7,8},{8,9},{9,10},{10,1... | collective-permute-start | bytes 3104 | tf_op jit(solution)/shard_map/ppermute | solution.py:22
  63.2 5.0 %collective-permute-start.10 = (f32[1,512]{1,0:T(1,128)S(1)}, f32[1,512]{1,0:T(1,128)S(1)}, u32[]{:S(2)}, u32[]{:S(2)}) collective-permute-start(f32[1,512]{1,0:T(1,128)S(1)} %get-tuple-element.24), channel_id=1, source_target_pairs={{16,0},{32,16},{48,32},{64,48},{80,64},{96,80},{112,96},{17,1},{33... | collective-permute-start | bytes 6152 | tf_op jit(solution)/shard_map/ppermute | solution.py:23
  65.1 4.9 collective-permute-start.11
  70.1 11.9 %collective-permute-start.12 = (f32[258,1]{1,0:T(8,128)S(1)}, f32[258,1]{1,0:T(8,128)S(1)}, u32[]{:S(2)}, u32[]{:S(2)}) collective-permute-start(f32[258,1]{1,0:T(8,128)S(1)} %get-tuple-element.13), channel_id=1, source_target_pairs={{1,0},{2,1},{3,2},{4,3},{5,4},{6,5},{7,6},{8,7},{9,8},{10,9},{11,1... | collective-permute-start | bytes 3104 | tf_op jit(solution)/shard_map/ppermute | solution.py:23
  72.1 10.0 %collective-permute-start.13 = (f32[258,1]{1,0:T(8,128)S(1)}, f32[258,1]{1,0:T(8,128)S(1)}, u32[]{:S(2)}, u32[]{:S(2)}) collective-permute-start(f32[258,1]{1,0:T(8,128)S(1)} %get-tuple-element.14), channel_id=1, source_target_pairs={{0,1},{1,2},{2,3},{3,4},{4,5},{5,6},{6,7},{7,8},{8,9},{9,10},{10,1... | collective-permute-start | bytes 3104 | tf_op jit(solution)/shard_map/ppermute | solution.py:22
  76.1 54.5 %collective-permute-start.16 = (f32[130,1]{1,0:T(8,128)S(1)}, f32[130,1]{1,0:T(8,128)S(1)}, u32[]{:S(2)}, u32[]{:S(2)}) collective-permute-start(f32[130,1]{1,0:T(8,128)S(1)} %get-tuple-element.37), channel_id=1, source_target_pairs={{1,0},{2,1},{3,2},{4,3},{5,4},{6,5},{7,6},{8,7},{9,8},{10,9},{11,1... | collective-permute-start | bytes 1568 | tf_op jit(solution)/shard_map/ppermute | solution.py:23
  80.1 50.5 %collective-permute-start.17 = (f32[130,1]{1,0:T(8,128)S(1)}, f32[130,1]{1,0:T(8,128)S(1)}, u32[]{:S(2)}, u32[]{:S(2)}) collective-permute-start(f32[130,1]{1,0:T(8,128)S(1)} %get-tuple-element.38), channel_id=1, source_target_pairs={{0,1},{1,2},{2,3},{3,4},{4,5},{5,6},{6,7},{7,8},{8,9},{9,10},{10,1... | collective-permute-start | bytes 1568 | tf_op jit(solution)/shard_map/ppermute | solution.py:22
  131.5 4.3 collective-permute-start.18
  133.4 4.9 collective-permute-start.19
  138.4 8.0 %collective-permute-start.20 = (f32[130,1]{1,0:T(8,128)S(1)}, f32[130,1]{1,0:T(8,128)S(1)}, u32[]{:S(2)}, u32[]{:S(2)}) collective-permute-start(f32[130,1]{1,0:T(8,128)S(1)} %get-tuple-element.35), channel_id=1, source_target_pairs={{1,0},{2,1},{3,2},{4,3},{5,4},{6,5},{7,6},{8,7},{9,8},{10,9},{11,1... | collective-permute-start | bytes 1568 | tf_op jit(solution)/shard_map/ppermute | solution.py:23
  144.5 8.3 %collective-permute-start.21 = (f32[130,1]{1,0:T(8,128)S(1)}, f32[130,1]{1,0:T(8,128)S(1)}, u32[]{:S(2)}, u32[]{:S(2)}) collective-permute-start(f32[130,1]{1,0:T(8,128)S(1)} %get-tuple-element.36), channel_id=1, source_target_pairs={{0,1},{1,2},{2,3},{3,4},{4,5},{5,6},{6,7},{7,8},{8,9},{9,10},{10,1... | collective-permute-start | bytes 1568 | tf_op jit(solution)/shard_map/ppermute | solution.py:22
  153.0 4.3 collective-permute-start.22
  154.9 4.9 collective-permute-start.23
  159.9 6.2 %collective-permute-start.24 = (f32[130,1]{1,0:T(8,128)S(1)}, f32[130,1]{1,0:T(8,128)S(1)}, u32[]{:S(2)}, u32[]{:S(2)}) collective-permute-start(f32[130,1]{1,0:T(8,128)S(1)} %get-tuple-element.33), channel_id=1, source_target_pairs={{1,0},{2,1},{3,2},{4,3},{5,4},{6,5},{7,6},{8,7},{9,8},{10,9},{11,1... | collective-permute-start | bytes 1568 | tf_op jit(solution)/shard_map/ppermute | solution.py:23
  161.8 8.3 %collective-permute-start.25 = (f32[130,1]{1,0:T(8,128)S(1)}, f32[130,1]{1,0:T(8,128)S(1)}, u32[]{:S(2)}, u32[]{:S(2)}) collective-permute-start(f32[130,1]{1,0:T(8,128)S(1)} %get-tuple-element.34), channel_id=1, source_target_pairs={{0,1},{1,2},{2,3},{3,4},{4,5},{5,6},{6,7},{7,8},{8,9},{9,10},{10,1... | collective-permute-start | bytes 1568 | tf_op jit(solution)/shard_map/ppermute | solution.py:22
  348.3 42.6 %slice-start = ((s8[16777216]{0:T(1024)(128)(4,1)}), s8[4194304]{0:T(1024)(128)(4,1)S(1)}, s32[]{:S(2)}) async-start(s8[16777216]{0:T(1024)(128)(4,1)} %bitcast.13), calls=%async_computation.1 | async-start | bytes 8388608
  348.3 42.6 %slice-start.1 = ((s8[16777216]{0:T(1024)(128)(4,1)}), s8[4194304]{0:T(1024)(128)(4,1)S(1)}, s32[]{:S(2)}) async-start(s8[16777216]{0:T(1024)(128)(4,1)} %bitcast.13), calls=%async_computation.2 | async-start | bytes 8388608
  348.3 42.6 %slice-start.2 = ((s8[16777216]{0:T(1024)(128)(4,1)}), s8[4194304]{0:T(1024)(128)(4,1)S(1)}, s32[]{:S(2)}) async-start(s8[16777216]{0:T(1024)(128)(4,1)} %bitcast.13), calls=%async_computation.3 | async-start | bytes 8388608
  378.9 12.0 %slice-start.3 = ((s8[16777216]{0:T(1024)(128)(4,1)}), s8[4194304]{0:T(1024)(128)(4,1)S(1)}, s32[]{:S(2)}) async-start(s8[16777216]{0:T(1024)(128)(4,1)} %bitcast.13), calls=%async_computation.4 | async-start | bytes 8388608
  419.0 4.3 collective-permute-start.26
  421.0 4.9 collective-permute-start.27
  425.9 6.5 %collective-permute-start.28 = (f32[130,1]{1,0:T(8,128)S(1)}, f32[130,1]{1,0:T(8,128)S(1)}, u32[]{:S(2)}, u32[]{:S(2)}) collective-permute-start(f32[130,1]{1,0:T(8,128)S(1)} %get-tuple-element.31), channel_id=1, source_target_pairs={{1,0},{2,1},{3,2},{4,3},{5,4},{6,5},{7,6},{8,7},{9,8},{10,9},{11,1... | collective-permute-start | bytes 1568 | tf_op jit(solution)/shard_map/ppermute | solution.py:23
  430.6 8.3 %collective-permute-start.29 = (f32[130,1]{1,0:T(8,128)S(1)}, f32[130,1]{1,0:T(8,128)S(1)}, u32[]{:S(2)}, u32[]{:S(2)}) collective-permute-start(f32[130,1]{1,0:T(8,128)S(1)} %get-tuple-element.32), channel_id=1, source_target_pairs={{0,1},{1,2},{2,3},{3,4},{4,5},{5,6},{6,7},{7,8},{8,9},{9,10},{10,1... | collective-permute-start | bytes 1568 | tf_op jit(solution)/shard_map/ppermute | solution.py:22
  439.1 4.3 collective-permute-start.30
  441.0 4.9 collective-permute-start.31
  446.0 6.2 %collective-permute-start.32 = (f32[130,1]{1,0:T(8,128)S(1)}, f32[130,1]{1,0:T(8,128)S(1)}, u32[]{:S(2)}, u32[]{:S(2)}) collective-permute-start(f32[130,1]{1,0:T(8,128)S(1)} %get-tuple-element.29), channel_id=1, source_target_pairs={{1,0},{2,1},{3,2},{4,3},{5,4},{6,5},{7,6},{8,7},{9,8},{10,9},{11,1... | collective-permute-start | bytes 1568 | tf_op jit(solution)/shard_map/ppermute | solution.py:23
  447.9 8.3 %collective-permute-start.33 = (f32[130,1]{1,0:T(8,128)S(1)}, f32[130,1]{1,0:T(8,128)S(1)}, u32[]{:S(2)}, u32[]{:S(2)}) collective-permute-start(f32[130,1]{1,0:T(8,128)S(1)} %get-tuple-element.30), channel_id=1, source_target_pairs={{0,1},{1,2},{2,3},{3,4},{4,5},{5,6},{6,7},{7,8},{8,9},{9,10},{10,1... | collective-permute-start | bytes 1568 | tf_op jit(solution)/shard_map/ppermute | solution.py:22
  457.7 4.3 collective-permute-start.34
  459.6 4.9 collective-permute-start.35
  464.7 6.9 %collective-permute-start.36 = (f32[258,1]{1,0:T(8,128)S(1)}, f32[258,1]{1,0:T(8,128)S(1)}, u32[]{:S(2)}, u32[]{:S(2)}) collective-permute-start(f32[258,1]{1,0:T(8,128)S(1)} %get-tuple-element.11), channel_id=1, source_target_pairs={{1,0},{2,1},{3,2},{4,3},{5,4},{6,5},{7,6},{8,7},{9,8},{10,9},{11,1... | collective-permute-start | bytes 3104 | tf_op jit(solution)/shard_map/ppermute | solution.py:23
  466.6 9.0 %collective-permute-start.37 = (f32[258,1]{1,0:T(8,128)S(1)}, f32[258,1]{1,0:T(8,128)S(1)}, u32[]{:S(2)}, u32[]{:S(2)}) collective-permute-start(f32[258,1]{1,0:T(8,128)S(1)} %get-tuple-element.12), channel_id=1, source_target_pairs={{0,1},{1,2},{2,3},{3,4},{4,5},{5,6},{6,7},{7,8},{8,9},{9,10},{10,1... | collective-permute-start | bytes 3104 | tf_op jit(solution)/shard_map/ppermute | solution.py:22
  476.2 4.3 collective-permute-start.38
  478.1 4.9 collective-permute-start.39
  483.1 6.9 %collective-permute-start.40 = (f32[258,1]{1,0:T(8,128)S(1)}, f32[258,1]{1,0:T(8,128)S(1)}, u32[]{:S(2)}, u32[]{:S(2)}) collective-permute-start(f32[258,1]{1,0:T(8,128)S(1)} %get-tuple-element.9), channel_id=1, source_target_pairs={{1,0},{2,1},{3,2},{4,3},{5,4},{6,5},{7,6},{8,7},{9,8},{10,9},{11,1... | collective-permute-start | bytes 3104 | tf_op jit(solution)/shard_map/ppermute | solution.py:23
  485.1 9.0 %collective-permute-start.41 = (f32[258,1]{1,0:T(8,128)S(1)}, f32[258,1]{1,0:T(8,128)S(1)}, u32[]{:S(2)}, u32[]{:S(2)}) collective-permute-start(f32[258,1]{1,0:T(8,128)S(1)} %get-tuple-element.10), channel_id=1, source_target_pairs={{0,1},{1,2},{2,3},{3,4},{4,5},{5,6},{6,7},{7,8},{8,9},{9,10},{10,1... | collective-permute-start | bytes 3104 | tf_op jit(solution)/shard_map/ppermute | solution.py:22
Sparse Core Ops, SparseCore 0:
  210.0 31.1 all-gather.1
where the time goes:
time: 511 us; the launch traced here: 503 us
  other arithmetic  156 us (31%)
  starting transfers between devices  113 us (22%)
  matrix products  83.2 us (16%)
  waiting for transfers between devices  62.3 us (12%)
  local copies, waits for them, and re-layouts  48 us (9%)
  blocking collectives  25.2 us (5%)
  between operations  14.9 us (3%)
    dot_general x1, other arithmetic, gathered_solve(): jnp.dot(jnp.dot(row_table.T, modes / lam, precision=hp), col_table, preci...  62.8 us
    dot_general x1, other arithmetic, gathered_solve(): jnp.dot(jnp.dot(row_table, whole, precision=hp), col_table.T, precision=hp)  62.5 us
    ppermute x20, waiting for transfers between devices, with_halo(): before = lax.ppermute(last, axis, up)  58.4 us
    ppermute x20, starting transfers between devices, with_halo(): after = lax.ppermute(first, axis, down)  54.2 us
    ppermute x20, starting transfers between devices, with_halo(): before = lax.ppermute(last, axis, up)  53 us
    reshape x2, local copies, waits for them, and re-layouts, restrict(): return field.reshape(nrows // 2, 2, ncols // 2, 2).sum(axis=(1, 3)) * 0.25  44.6 us
    dot_general x1, matrix products, gathered_solve(): jnp.dot(jnp.dot(row_table, whole, precision=hp), col_table.T, precision=hp)  30.6 us
    dot_general x1, matrix products, gathered_solve(): jnp.dot(jnp.dot(row_table.T, modes / lam, precision=hp), col_table, preci...  27.7 us
  transfers between devices with their start and end apart: 43, of which 21 were waited for; matrix products, arithmetic and copies ran while one was open for 36% of the time, Pallas kernels for 0%

commit v1 on v0

v1 whole, which is shorter than its diff:
```python
import functools
import math

import jax
import jax.numpy as jnp
import ml_dtypes
import numpy as np
from jax import lax
from jax.experimental import pallas as pl
from jax.experimental.pallas import tpu as pltpu
from jax.sharding import PartitionSpec as P

MESH = pl.DeviceIdType.MESH
SCREEN = 4e-06
OMEGA = 0.8
NR, NC = 8, 16
H0, W0 = 256, 512
QR, QC = 64, 128
ER, EC = 72, 256
BF, F32 = jnp.bfloat16, jnp.float32


def bf16_parts(x, parts):
    out = []
    rest = np.asarray(x, np.float64)
    for _ in range(parts):
        piece = rest.astype(ml_dtypes.bfloat16)
        out.append(piece)
        rest = rest - piece.astype(np.float64)
    return out


@functools.lru_cache(maxsize=None)
def tables():
    rows, cols = NR * QR, NC * QC
    perm = np.zeros((W0, W0), np.float32)
    q = np.arange(QC)
    for pc in range(4):
        perm[4 * q + pc, pc * QC + q] = 1
    side = np.zeros((128, W0), np.float32)
    for pc in range(4):
        for s in range(4):
            side[112 + 4 * s + pc, pc * 128 + 124 + s] = 1
            side[4 * s + pc, pc * 128 + s] = 1
    k = np.arange(rows)
    place = np.arange(rows)
    phase = ((2 * place[:, None] + 1) * k[None, :]) % (4 * rows)
    scale = np.where(k == 0, math.sqrt(1.0 / rows), math.sqrt(2.0 / rows))
    ct = np.zeros((rows + 32, rows))
    ct[16:-16] = scale[None, :] * np.cos(phase * (math.pi / (2 * rows)))
    ct = np.stack(bf16_parts(ct, 3))
    mu = SCREEN + 0.25 * 4 * np.sin(np.pi * k / (2 * rows)) ** 2
    half = 1 + 2 * mu
    rho = half - np.sqrt(4 * mu + 4 * mu * mu)
    g0 = 1 / (0.25 * (1 / rho - rho))
    t = np.arange(QC)
    from_left = rho[None, :] ** (t[:, None] + 1)
    from_right = rho[None, :] ** (QC - t[:, None])
    small = np.zeros((16, rows))
    for i in range(7):
        small[i] = rho ** (2**i)
    small[7] = g0
    small[8] = g0 * rho
    small[9] = rho ** (QC + 1)
    small[10] = 2 + 4 * mu
    tab = np.concatenate([from_left, from_right, small]).astype(np.float32)
    dist = g0 / (1 - rho ** (2 * cols)) * rho ** (QC * np.arange(32)[:, None])
    dist = dist.reshape(32, 4, 128)
    dist = np.concatenate([dist, dist], axis=1).astype(np.float32)
    return (
        perm.astype(ml_dtypes.bfloat16),
        perm.T.astype(ml_dtypes.bfloat16),
        side.astype(ml_dtypes.bfloat16),
        ct,
        tab,
        dist,
    )


def split2(x):
    hi = x.astype(BF)
    return hi, (x - hi.astype(F32)).astype(BF)


def split3(x):
    hi = x.astype(BF)
    rest = x - hi.astype(F32)
    mid = rest.astype(BF)
    return hi, mid, (rest - mid.astype(F32)).astype(BF)


def mm(a, b, dims=((1,), (0,))):
    return lax.dot_general(a, b, (dims, ((), ())), preferred_element_type=F32)


def permuted(x, table):
    hi, mid = split2(x)
    return mm(hi, table) + mm(mid, table)


def roll(x, shift, axis):
    return pltpu.roll(x, shift % x.shape[axis], axis)


def around(ref, pr, pc, n):
    up = ref[(pr - 1) * n + pc] if pr > 0 else roll(ref[(n - 1) * n + pc], 1, 0)
    down = ref[(pr + 1) * n + pc] if pr < n - 1 else roll(ref[pc], -1, 0)
    left = ref[pr * n + pc - 1] if pc > 0 else roll(ref[pr * n + n - 1], 1, 1)
    right = ref[pr * n + pc + 1] if pc < n - 1 else roll(ref[pr * n], -1, 1)
    return (up + down) + (left + right)


def klass(p, n):
    return 0 if p == 0 else (2 if p == n - 1 else 1)


def which(pr, pc, n):
    return 3 * klass(pr, n) + klass(pc, n)


def sweep(src, dst, f, w, n, c):
    for pr in range(n):
        for pc in range(n):
            i = pr * n + pc
            nb = around(src, pr, pc, n)
            nb = nb if c == 1.0 else c * nb
            dst[i] = (1 - OMEGA) * src[i] + w[which(pr, pc, n)] * (f[i] + nb)


def kernel(
    lum_h, gx_h, gy_h, lab_h, perm_h, permt_h, side_h, ct_h, tab_h, dist_h,
    out_h,
    gx, gy, lab, raw, perm, permt, side, ct, tab, dist,
    to_right, to_left, from_l, from_r, corner_l, corner_r,
    lum, selx, sely, rhs, fa, fb, w0, d0, w1, d1, f1, ea, eb, ec,
    strip, mom, xs, out,
    in_sem, const_sem, out_sem, h_send, h_recv, r_send, r_recv, c_send, c_recv,
):
    r = lax.axis_index("rows")
    c = lax.axis_index("cols")

    def row_peer(d):
        return lax.rem(r + d + NR, NR)

    def col_peer(d):
        return lax.rem(c + d + NC, NC)

    barrier = pltpu.get_barrier_semaphore()
    peers = [(d, 0) for d in range(1, NR)] + [(0, d) for d in range(1, NC)]
    peers += [(1, 1), (1, -1), (-1, 1), (-1, -1)]
    for dr, dc in peers:
        pl.semaphore_signal(
            barrier, inc=1, device_id=(row_peer(dr), col_peer(dc)), device_id_type=MESH
        )

    CH = 64
    loads = []
    for i in range(H0 // CH):
        rows = pl.ds(i * CH, CH)
        loads.append([
            pltpu.make_async_copy(gx_h.at[:, rows], gx.at[:, rows], in_sem.at[i, 0]),
            pltpu.make_async_copy(gy_h.at[:, rows], gy.at[:, rows], in_sem.at[i, 1]),
            pltpu.make_async_copy(lab_h.at[rows], lab.at[rows], in_sem.at[i, 2]),
        ] + [
            pltpu.make_async_copy(lum_h.at[rows, pl.ds(t * 128, 128)], raw.at[0, t, rows], in_sem.at[i, 3 + t])
            for t in range(4)
        ])
    for group in loads:
        for one in group:
            one.start()
    consts = [
        pltpu.make_async_copy(a, b, const_sem.at[i])
        for i, (a, b) in enumerate(
            [(perm_h, perm), (side_h, side), (ct_h, ct), (tab_h, tab), (dist_h, dist), (permt_h, permt)]
        )
    ]
    for one in consts:
        one.start()

    ri = lax.broadcasted_iota(jnp.int32, (ER, EC), 0)
    li = lax.broadcasted_iota(jnp.int32, (ER, EC), 1)
    out_rows = ((r == 0) & (ri >= 68)) | ((r == NR - 1) & (ri >= 64) & (ri < 68))
    out_cols = ((c == 0) & (li >= 192)) | ((c == NC - 1) & (li >= 128) & (li < 192))
    inside = jnp.where(out_rows | out_cols, 0.0, 1.0).astype(F32)
    edge_rows = [((r == 0) & (ri == 0)), None, ((r == NR - 1) & (ri == QR - 1))]
    edge_cols = [((c == 0) & (li == 0)), None, ((c == NC - 1) & (li == QC - 1))]
    for a in range(3):
        for b in range(3):
            deg = jnp.full((ER, EC), 4.0, F32)
            if a != 1:
                deg = deg - jnp.where(edge_rows[a], 1.0, 0.0)
            if b != 1:
                deg = deg - jnp.where(edge_cols[b], 1.0, 0.0)
            for wr, dr_, coef in ((w0, d0, 1.0), (w1, d1, 0.5)):
                if coef == 0.5 and (a == 1 or b == 1):
                    continue
                dr_[3 * a + b] = coef * deg
                wr[3 * a + b] = inside * (OMEGA / (SCREEN + coef * deg))
    xs[...] = jnp.zeros_like(xs)

    lane8 = lax.broadcasted_iota(jnp.int32, (8, W0), 1)
    sub8 = lax.broadcasted_iota(jnp.int32, (8, W0), 0)
    last_col = (c == NC - 1) & (lane8 == W0 - 1)
    for i in range(H0 // CH):
        for one in loads[i]:
            one.wait()

        def select(s, carry, i=i):
            row = pl.multiple_of(i * CH + s * 8, 8)
            rows = pl.ds(row, 8)
            lb = lab[rows, :]
            is0, is1, is2 = lb == 0, lb == 1, lb == 2
            sx = jnp.where(is0, gx[0, rows, :], jnp.where(is1, gx[1, rows, :], jnp.where(is2, gx[2, rows, :], gx[3, rows, :])))
            sy = jnp.where(is0, gy[0, rows, :], jnp.where(is1, gy[1, rows, :], jnp.where(is2, gy[2, rows, :], gy[3, rows, :])))
            sx = jnp.where(last_col, 0.0, sx)
            last_row = (r == NR - 1) & (sub8 + row == H0 - 1)
            sy = jnp.where(last_row, 0.0, sy)
            for t in range(4):
                raw[1, t, rows, :] = sx[:, t * 128:(t + 1) * 128]
                raw[2, t, rows, :] = sy[:, t * 128:(t + 1) * 128]
            return carry

        lax.fori_loop(0, CH // 8, select, 0, unroll=2)

    lane = lax.broadcasted_iota(jnp.int32, (QR, 128), 1)
    group = lane // 16
    for tile in range(2):
        packed_r = jnp.zeros((QR, 128), F32)
        packed_l = jnp.zeros((QR, 128), F32)
        for g in range(8):
            idx = tile * 8 + g
            if idx >= 12:
                break
            a, rp = divmod(idx, 4)
            edge = raw[a, 3, pl.ds(rp, QR, stride=4), :]
            packed_r = jnp.where(group == g, roll(edge, 16 * g - 112, 1), packed_r)
            edge = raw[a, 0, pl.ds(rp, QR, stride=4), :]
            packed_l = jnp.where(group == g, roll(edge, 16 * g, 1), packed_l)
        to_right[:, pl.ds(tile * 128, 128)] = packed_r
        to_left[:, pl.ds(tile * 128, 128)] = packed_l

    pl.semaphore_wait(barrier, len(peers))

    top, bottom = pl.ds(0, 16), pl.ds(H0 - 16, 16)
    halo = []
    for i, (src, dst, dr, dc) in enumerate([
        (to_right, from_l, 0, 1),
        (to_left, from_r, 0, -1),
        (raw.at[:, :, bottom], raw.at[:, :, pl.ds(H0 + 16, 16)], 1, 0),
        (raw.at[:, :, top], raw.at[:, :, pl.ds(H0, 16)], -1, 0),
        (raw.at[:, 3, bottom], corner_l.at[:, pl.ds(16, 16)], 1, 1),
        (raw.at[:, 0, bottom], corner_r.at[:, pl.ds(16, 16)], 1, -1),
        (raw.at[:, 3, top], corner_l.at[:, pl.ds(0, 16)], -1, 1),
        (raw.at[:, 0, top], corner_r.at[:, pl.ds(0, 16)], -1, -1),
    ]):
        copy = pltpu.make_async_remote_copy(
            src_ref=src, dst_ref=dst, send_sem=h_send.at[i], recv_sem=h_recv.at[i],
            device_id=(row_peer(dr), col_peer(dc)), device_id_type=MESH,
        )
        copy.start()
        halo.append(copy)

    fields = (lum, selx, sely)

    def by_phase(a, rows):
        return jnp.concatenate([raw[a, t, rows, :] for t in range(4)], axis=1)

    consts[0].wait()
    consts[1].wait()
    for a in range(3):
        x = jnp.concatenate([by_phase(a, pl.ds(rp, QR, stride=4)) for rp in range(4)], axis=0)
        y = permuted(x, perm[...])
        for rp in range(4):
            for pc in range(4):
                fields[a][rp * 4 + pc, pl.ds(0, QR), pl.ds(0, 128)] = y[rp * QR:(rp + 1) * QR, pc * 128:(pc + 1) * 128]

    for copy in halo:
        copy.wait()
    x = jnp.concatenate([by_phase(a, pl.ds(H0 + rp, 8, stride=4)) for a in range(3) for rp in range(4)], axis=0)
    y = permuted(x, perm[...])
    for a in range(3):
        for rp in range(4):
            i = (a * 4 + rp) * 8
            for pc in range(4):
                fields[a][rp * 4 + pc, pl.ds(QR, 8), pl.ds(0, 128)] = y[i:i + 8, pc * 128:(pc + 1) * 128]
    lane8 = lax.broadcasted_iota(jnp.int32, (8, 128), 1)
    for a in range(3):
        pieces = []
        for rp in range(4):
            tile, g = divmod(a * 4 + rp, 8)
            fl = roll(from_l[:, pl.ds(tile * 128, 128)], 112 - 16 * g, 1)
            fr = roll(from_r[:, pl.ds(tile * 128, 128)], -16 * g, 1)
            pieces.append(jnp.where(lane < 64, fr, fl))
            pieces.append(jnp.where(
                lane8 < 64,
                corner_r[a, pl.ds(rp, 8, stride=4), :],
                corner_l[a, pl.ds(rp, 8, stride=4), :],
            ))
        y = permuted(jnp.concatenate(pieces, axis=0), side[...])
        for rp in range(4):
            for pc in range(4):
                fields[a][rp * 4 + pc, :, pl.ds(128, 128)] = y[rp * ER:(rp + 1) * ER, pc * 128:(pc + 1) * 128]

    for i in range(16):
        lum[i] = lum[i] * inside
        if i % 4 == 3:
            selx[i] = selx[i] * inside
        if i // 4 == 3:
            sely[i] = sely[i] * inside
    for pr in range(4):
        for pc in range(4):
            i = pr * 4 + pc
            left = selx[i - 1] if pc > 0 else roll(selx[pr * 4 + 3], 1, 1)
            up = sely[i - 4] if pr > 0 else roll(sely[12 + pc], 1, 0)
            rhs[i] = SCREEN * lum[i] + (left - selx[i]) + (up - sely[i])

    sweep(lum, fa, rhs, w0, 4, 1.0)
    sweep(fa, fb, rhs, w0, 4, 1.0)
    for a in range(2):
        for b in range(2):
            total = None
            for pr in (2 * a, 2 * a + 1):
                for pc in (2 * b, 2 * b + 1):
                    i = pr * 4 + pc
                    res = (rhs[i] - SCREEN * fb[i]) + (around(fb, pr, pc, 4) - d0[which(pr, pc, 4)] * fb[i])
                    total = res if total is None else total + res
            f1[a * 2 + b] = 0.25 * total
            ea[a * 2 + b] = w1[which(a, b, 2)] * (0.25 * total)
    sweep(ea, eb, f1, w1, 2, 0.5)
    total = None
    for a in range(2):
        for b in range(2):
            i = a * 2 + b
            res = (f1[i] - SCREEN * eb[i]) + (0.5 * around(eb, a, b, 2) - d1[which(a, b, 2)] * eb[i])
            total = res if total is None else total + res
    strip[r] = 0.25 * total[0:QR, 0:QC]

    copies = []
    for d in range(1, NR):
        copy = pltpu.make_async_remote_copy(
            src_ref=strip.at[r], dst_ref=strip.at[r], send_sem=r_send.at[d], recv_sem=r_recv.at[d],
            device_id=(row_peer(d), c), device_id_type=MESH,
        )
        copy.start()
        copies.append(copy)
    for one in consts[2:]:
        one.wait()
    for copy in copies:
        copy.wait()

    whole = strip[...].reshape(NR * QR, QC)
    xh, xm, xl = split3(whole.T)
    inner = pl.ds(16, NR * QR)
    ch, cm, cl = ct[0, inner, :], ct[1, inner, :], ct[2, inner, :]
    g = mm(xh, ch) + ((mm(xh, cm) + mm(xm, ch)) + (mm(xm, cm) + (mm(xh, cl) + mm(xl, ch))))

    def small(i):
        return tab[pl.ds(2 * QC + i, 1), :]

    jrow = lax.broadcasted_iota(jnp.int32, (QC, NR * QR), 0)
    fwd, bwd = g, g
    for i, s in enumerate((1, 2, 4, 8, 16, 32, 64)):
        p = small(i)
        fwd = fwd + jnp.where(jrow >= s, roll(fwd, s, 0) * p, 0.0)
        bwd = bwd + jnp.where(jrow < QC - s, roll(bwd, -s, 0) * p, 0.0)
    lines = [fwd[QC - 1:QC], bwd[0:1], g[0:1], g[QC - 1:QC]]
    mom[c] = jnp.concatenate([x[:, t * 128:(t + 1) * 128] for x in lines for t in range(4)], axis=0)

    copies = []
    for d in range(1, NC):
        part = pl.ds(0, 16 if d in (1, NC - 1) else 8)
        copy = pltpu.make_async_remote_copy(
            src_ref=mom.at[c, part], dst_ref=mom.at[c, part], send_sem=c_send.at[d], recv_sem=c_recv.at[d],
            device_id=(r, col_peer(d)), device_id_type=MESH,
        )
        copy.start()
        copies.append(copy)
    own = small(7) * (fwd + bwd - g)
    for copy in copies:
        copy.wait()

    low = lax.broadcasted_iota(jnp.int32, (8, 128), 0) < 4
    sum_a = jnp.zeros((8, 128), F32)
    sum_b = jnp.zeros((8, 128), F32)
    for o in range(NC):
        m = mom[o, pl.ds(0, 8), :]
        sum_a = sum_a + m * jnp.where(low, dist[lax.rem(c - o + 63, 32)], dist[c + o])
        sum_b = sum_b + m * jnp.where(low, dist[lax.rem(62 - c - o, 32)], dist[lax.rem(o - c + 63, 32)])

    def as_row(x):
        x = x[0:4] + x[4:8]
        return jnp.concatenate([x[t:t + 1] for t in range(4)], axis=1)

    def line(o, i):
        x = mom[o, pl.ds(8, 8), :]
        return jnp.concatenate([x[4 * i + t:4 * i + t + 1] for t in range(4)], axis=1)

    a_in, b_in = as_row(sum_a), as_row(sum_b)
    own = own + tab[pl.ds(0, QC), :] * a_in + tab[pl.ds(QC, QC), :] * b_in
    xs[pl.ds(0, QC), :] = own
    left1 = a_in + small(8) * lines[1] + small(9) * b_in
    right1 = b_in + small(8) * lines[0] + small(9) * a_in
    left2 = small(10) * left1 - own[0:1] - 4.0 * line(col_peer(-1), 1)
    right2 = small(10) * right1 - own[QC - 1:QC] - 4.0 * line(col_peer(1), 0)
    zero6 = jnp.zeros((6, NR * QR), F32)
    xs[pl.ds(QC, 8), :] = jnp.concatenate([right1, right2, zero6], axis=0)
    xs[pl.ds(EC - 8, 8), :] = jnp.concatenate([zero6, left2, left1], axis=0)

    base = pl.multiple_of(r * QR, QR)
    sub16 = lax.broadcasted_iota(jnp.int32, (16, NR * QR), 0)
    back = []
    for i in range(3):
        tail = jnp.where(
            sub16 < 8,
            ct[i, pl.ds(base + QR + 16, 16), :].astype(F32),
            ct[i, pl.ds(base, 16), :].astype(F32),
        ).astype(BF)
        back.append(jnp.concatenate([ct[i, pl.ds(base + 16, QR), :], tail], axis=0))
    th, tm, tl = back
    xh, xm, xl = split3(xs[...])
    nt = ((1,), (1,))
    e2 = mm(th, xh, nt) + ((mm(th, xm, nt) + mm(tm, xh, nt)) + (mm(tm, xm, nt) + (mm(th, xl, nt) + mm(tl, xh, nt))))
    sub8 = lax.broadcasted_iota(jnp.int32, (8, EC), 0)
    e2 = jnp.concatenate([e2[0:QR], jnp.where(sub8 < 4, e2[QR:QR + 8], e2[QR + 8:QR + 16])], axis=0)
    e2 = e2 * inside

    for i in range(4):
        ea[i] = eb[i] + e2
    sweep(ea, ec, f1, w1, 2, 0.5)
    sweep(ec, ea, f1, w1, 2, 0.5)
    for pr in range(4):
        for pc in range(4):
            fa[pr * 4 + pc] = fb[pr * 4 + pc] + ea[(pr // 2) * 2 + pc // 2]
    sweep(fa, lum, rhs, w0, 4, 1.0)
    sweep(lum, fb, rhs, w0, 4, 1.0)
    x = jnp.concatenate([
        jnp.concatenate([fb[pr * 4 + pc, pl.ds(0, QR), pl.ds(0, QC)] for pc in range(4)], axis=1)
        for pr in range(4)
    ], axis=0)
    y = permuted(x, permt[...])
    for pr in range(4):
        for t in range(4):
            out[t, pl.ds(pr, QR, stride=4), :] = y[pr * QR:(pr + 1) * QR, t * 128:(t + 1) * 128]
    copies = [
        pltpu.make_async_copy(out.at[t], out_h.at[:, pl.ds(t * 128, 128)], out_sem.at[t]) for t in range(4)
    ]
    for copy in copies:
        copy.start()
    for copy in copies:
        copy.wait()


def shards(luminance, grad_x, grad_y, labels):
    consts = tables()
    vmem = pltpu.VMEM
    phases = vmem((16, ER, EC), F32)
    quarter = vmem((4, ER, EC), F32)
    nine = vmem((9, ER, EC), F32)
    dma = pltpu.SemaphoreType.DMA
    return pl.pallas_call(
        kernel,
        out_shape=jax.ShapeDtypeStruct((H0, W0), F32),
        in_specs=[pl.BlockSpec(memory_space=pl.ANY)] * 10,
        out_specs=pl.BlockSpec(memory_space=pl.ANY),
        scratch_shapes=[
            vmem((4, H0, W0), F32),
            vmem((4, H0, W0), F32),
            vmem((H0, W0), jnp.int32),
            vmem((3, 4, H0 + 32, 128), F32),
            vmem((W0, W0), BF),
            vmem((W0, W0), BF),
            vmem((128, W0), BF),
            vmem(consts[3].shape, BF),
            vmem(consts[4].shape, F32),
            vmem(consts[5].shape, F32),
            vmem((QR, 256), F32),
            vmem((QR, 256), F32),
            vmem((QR, 256), F32),
            vmem((QR, 256), F32),
            vmem((3, 32, 128), F32),
            vmem((3, 32, 128), F32),
            phases, phases, phases, phases, phases, phases,
            nine, nine, nine, nine,
            quarter, quarter, quarter, quarter,
            vmem((NR, QR, QC), F32),
            vmem((NC, 16, 128), F32),
            vmem((EC, NR * QR), F32),
            vmem((4, H0, 128), F32),
            dma((4, 7)),
            dma((6,)),
            dma((4,)),
            dma((8,)),
            dma((8,)),
            dma((NR,)),
            dma((NR,)),
            dma((NC,)),
            dma((NC,)),
        ],
        compiler_params=pltpu.CompilerParams(
            collective_id=0, has_side_effects=True, vmem_limit_bytes=56 * 1024 * 1024
        ),
    )(luminance, grad_x, grad_y, labels, *[jnp.asarray(x) for x in consts])


def solution(mesh):
    return jax.shard_map(
        shards,
        mesh=mesh,
        in_specs=(
            P("rows", "cols"),
            P(None, "rows", "cols"),
            P(None, "rows", "cols"),
            P("rows", "cols"),
        ),
        out_specs=P("rows", "cols"),
        check_vma=False,
    )
```

time: 511 us -> 33.7 us (0.07)
  the two profiles are of different devices: /device:TPU:12 before, /device:TPU:1 now
where the time goes in v1:
time: 33.7 us; the launch traced here: 33.5 us
  Pallas kernels  31.6 us (94%)
  local copies, waits for them, and re-layouts  1.87 us (6%)
    pallas_call x1, Pallas kernels, shards(): pl.pallas_call(kernel, out_shape=jax.ShapeDtypeStruct((H0, W0), F32), in_...  31.6 us
    unnamed x1, local copies, waits for them, and re-layouts  1.87 us

profile of v1, /device:TPU:1, one launch (start us, length us, event | category | flops | bytes accessed | tf_op | source)
XLA Modules:
  0.0 33.5 jit_solution(752883276948073200)
XLA Ops:
  0.0 31.6 %shard_map.100 = f32[256,512]{1,0:T(8,128)} custom-call(f32[256,512]{1,0:T(8,128)} %lum_h.1, f32[4,256,512]{2,1,0:T(8,128)} %gx_h.1, f32[4,256,512]{2,1,0:T(8,128)} %gy_h.1, s32[256,512]{1,0:T(8,128)} %lab_h.1, bf16[512,512]{1,0:T(8,128)(2,1)} %constant.12.clone.perm_h, bf16[512,512]{1,0:T(8,128)(2,1)} %constant.13.clone.permt_h, ...), custom_call_target="tpu_custom_call" | custom-call | tf_op jit(solution)/shard_map/pallas_call | solution.py:460
  31.6 1.9 %copy.12 = f32[256,512]{1,0:T(8,128)} copy(f32[256,512]{1,0:T(8,128)} %shard_map.100) | data formatting | bytes 1048576

commit v2 on v1

v2 whole, which is shorter than its diff:
```python
import functools
import math

import jax
import jax.numpy as jnp
import ml_dtypes
import numpy as np
from jax import lax
from jax.experimental import pallas as pl
from jax.experimental.pallas import tpu as pltpu
from jax.sharding import PartitionSpec as P

MESH = pl.DeviceIdType.MESH
SCREEN = 4e-06
OMEGA = 0.8
NR, NC = 8, 16
H0, W0 = 256, 512
QR, QC = 64, 128
ER, EC = 72, 256
BF, F32 = jnp.bfloat16, jnp.float32


def bf16_parts(x, parts):
    out = []
    rest = np.asarray(x, np.float64)
    for _ in range(parts):
        piece = rest.astype(ml_dtypes.bfloat16)
        out.append(piece)
        rest = rest - piece.astype(np.float64)
    return out


@functools.lru_cache(maxsize=None)
def tables():
    rows, cols = NR * QR, NC * QC
    k = np.arange(rows)
    place = np.arange(rows)
    phase = ((2 * place[:, None] + 1) * k[None, :]) % (4 * rows)
    scale = np.where(k == 0, math.sqrt(1.0 / rows), math.sqrt(2.0 / rows))
    ct = np.zeros((rows + 32, rows))
    ct[16:-16] = scale[None, :] * np.cos(phase * (math.pi / (2 * rows)))
    ct = np.stack(bf16_parts(ct, 3))
    mu = SCREEN + 0.25 * 4 * np.sin(np.pi * k / (2 * rows)) ** 2
    half = 1 + 2 * mu
    rho = half - np.sqrt(4 * mu + 4 * mu * mu)
    g0 = 1 / (0.25 * (1 / rho - rho))
    t = np.arange(QC)
    from_left = rho[None, :] ** (t[:, None] + 1)
    from_right = rho[None, :] ** (QC - t[:, None])
    small = np.zeros((16, rows))
    for i in range(7):
        small[i] = rho ** (2**i)
    small[7] = g0
    small[8] = g0 * rho
    small[9] = rho ** (QC + 1)
    small[10] = 2 + 4 * mu
    small[11] = rho**QC
    small[12] = 1 / rho
    small[13] = rho**-2.0
    tab = np.concatenate([from_left, from_right, small]).astype(np.float32)
    dist = g0 / (1 - rho ** (2 * cols)) * rho ** (QC * np.arange(32)[:, None])
    dist = dist.reshape(32, 4, 128)
    dist = np.concatenate([dist, dist], axis=1).astype(np.float32)
    return ct, tab, dist


def split2(x):
    hi = x.astype(BF)
    return hi, (x - hi.astype(F32)).astype(BF)


def split3(x):
    hi = x.astype(BF)
    rest = x - hi.astype(F32)
    mid = rest.astype(BF)
    return hi, mid, (rest - mid.astype(F32)).astype(BF)


def mm(a, b, dims=((1,), (0,))):
    return lax.dot_general(a, b, (dims, ((), ())), preferred_element_type=F32)


def permuted(x, table):
    hi, mid = split2(x)
    return mm(hi, table) + mm(mid, table)


def roll(x, shift, axis):
    return pltpu.roll(x, shift % x.shape[axis], axis)


def around(ref, pr, pc, n):
    up = ref[(pr - 1) * n + pc] if pr > 0 else roll(ref[(n - 1) * n + pc], 1, 0)
    down = ref[(pr + 1) * n + pc] if pr < n - 1 else roll(ref[pc], -1, 0)
    left = ref[pr * n + pc - 1] if pc > 0 else roll(ref[pr * n + n - 1], 1, 1)
    right = ref[pr * n + pc + 1] if pc < n - 1 else roll(ref[pr * n], -1, 1)
    return (up + down) + (left + right)


def klass(p, n):
    return 0 if p == 0 else (2 if p == n - 1 else 1)


def which(pr, pc, n):
    return 3 * klass(pr, n) + klass(pc, n)


def sweep(src, dst, f, w, n, c):
    for pr in range(n):
        for pc in range(n):
            i = pr * n + pc
            nb = around(src, pr, pc, n)
            nb = nb if c == 1.0 else c * nb
            dst[i] = (1 - OMEGA) * src[i] + w[which(pr, pc, n)] * (f[i] + nb)


def kernel(
    lum_h, gx_h, gy_h, lab_h, ct_h, tab_h, dist_h,
    out_h,
    gx, gy, lab, raw, perm, permt, side, ct, tab, dist,
    to_right, to_left, from_l, from_r,
    lum, selx, sely, rhs, fa, fb, w0, d0, w1, d1, f1, ea, eb, ec,
    strip, mom, xs, out,
    in_sem, const_sem, out_sem, h_send, h_recv, r_send, r_recv, c_send, c_recv,
):
    r = lax.axis_index("rows")
    c = lax.axis_index("cols")

    def row_peer(d):
        return lax.rem(r + d + NR, NR)

    def col_peer(d):
        return lax.rem(c + d + NC, NC)

    sibling = r + 1 - 2 * lax.rem(r, 2)
    barrier = pltpu.get_barrier_semaphore()
    peers = [(d, 0) for d in (1, 2, 4, 6, 7)] + [(0, d) for d in range(1, NC)]
    peers += [(1, 1), (1, -1), (-1, 1), (-1, -1)]
    for dr, dc in peers:
        pl.semaphore_signal(
            barrier, inc=1, device_id=(row_peer(dr), col_peer(dc)), device_id_type=MESH
        )

    CH = 64
    loads = []
    for i in range(H0 // CH):
        rows = pl.ds(i * CH, CH)
        loads.append([
            pltpu.make_async_copy(gx_h.at[:, rows], gx.at[:, rows], in_sem.at[i, 0]),
            pltpu.make_async_copy(gy_h.at[:, rows], gy.at[:, rows], in_sem.at[i, 1]),
            pltpu.make_async_copy(lab_h.at[rows], lab.at[rows], in_sem.at[i, 2]),
        ] + [
            pltpu.make_async_copy(lum_h.at[rows, pl.ds(t * 128, 128)], raw.at[0, t, rows], in_sem.at[i, 3 + t])
            for t in range(4)
        ])
    for group in loads:
        for one in group:
            one.start()
    consts = [
        pltpu.make_async_copy(a, b, const_sem.at[i])
        for i, (a, b) in enumerate([(ct_h, ct), (tab_h, tab), (dist_h, dist)])
    ]

    src = lax.broadcasted_iota(jnp.int32, (W0, 128), 0)
    dst = 4 * lax.broadcasted_iota(jnp.int32, (W0, 128), 1)
    back_src = 4 * lax.broadcasted_iota(jnp.int32, (128, W0), 0)
    back_dst = lax.broadcasted_iota(jnp.int32, (128, W0), 1)
    src_s = lax.broadcasted_iota(jnp.int32, (128, 128), 0)
    lane_s = lax.broadcasted_iota(jnp.int32, (128, 128), 1)
    outer = (lane_s < 4) | (lane_s >= 124)
    for pc in range(4):
        part = pl.ds(pc * 128, 128)
        perm[:, part] = jnp.where(src == dst + pc, 1.0, 0.0).astype(BF)
        permt[part, :] = jnp.where(back_src + pc == back_dst, 1.0, 0.0).astype(BF)
        side[:, part] = jnp.where(outer & (src_s == lax.rem(4 * lane_s + pc, 128)), 1.0, 0.0).astype(BF)

    ri = lax.broadcasted_iota(jnp.int32, (ER, EC), 0)
    li = lax.broadcasted_iota(jnp.int32, (ER, EC), 1)
    out_rows = ((r == 0) & (ri >= 68)) | ((r == NR - 1) & (ri >= 64) & (ri < 68))
    out_cols = ((c == 0) & (li >= 192)) | ((c == NC - 1) & (li >= 128) & (li < 192))
    inside = jnp.where(out_rows | out_cols, 0.0, 1.0).astype(F32)
    edge_rows = [((r == 0) & (ri == 0)), None, ((r == NR - 1) & (ri == QR - 1))]
    edge_cols = [((c == 0) & (li == 0)), None, ((c == NC - 1) & (li == QC - 1))]
    for a in range(3):
        for b in range(3):
            deg = jnp.full((ER, EC), 4.0, F32)
            if a != 1:
                deg = deg - jnp.where(edge_rows[a], 1.0, 0.0)
            if b != 1:
                deg = deg - jnp.where(edge_cols[b], 1.0, 0.0)
            for wr, dr_, coef in ((w0, d0, 1.0), (w1, d1, 0.5)):
                if coef == 0.5 and (a == 1 or b == 1):
                    continue
                dr_[3 * a + b] = coef * deg
                wr[3 * a + b] = inside * (OMEGA / (SCREEN + coef * deg))
    xs[...] = jnp.zeros_like(xs)
    fields = (lum, selx, sely)
    for field in fields:
        for i in range(16):
            field[i, pl.ds(QR, 8), pl.ds(0, QC)] = jnp.zeros((8, QC), F32)
            field[i, :, pl.ds(QC, 128)] = jnp.zeros((ER, 128), F32)

    lane8 = lax.broadcasted_iota(jnp.int32, (8, 128), 1)
    sub8 = lax.broadcasted_iota(jnp.int32, (8, 128), 0)
    for i in range(H0 // CH):
        for one in loads[i]:
            one.wait()

        def select(s, carry, i=i):
            row = pl.multiple_of(i * CH + s * 8, 8)
            rows = pl.ds(row, 8)
            last_row = (r == NR - 1) & (sub8 + row == H0 - 1)
            for t in range(4):
                cols = pl.ds(t * 128, 128)
                lb = lab[rows, cols]
                is0, is1, is2 = lb == 0, lb == 1, lb == 2

                def pick(g):
                    return jnp.where(is0, g[0, rows, cols], jnp.where(
                        is1, g[1, rows, cols], jnp.where(is2, g[2, rows, cols], g[3, rows, cols])))

                sx, sy = pick(gx), pick(gy)
                if t == 3:
                    sx = jnp.where((c == NC - 1) & (lane8 == 127), 0.0, sx)
                raw[1, t, rows, :] = sx
                raw[2, t, rows, :] = jnp.where(last_row, 0.0, sy)
            return carry

        lax.fori_loop(0, CH // 8, select, 0, unroll=2)
    for one in consts:
        one.start()

    def by_phase(a, rows):
        return jnp.concatenate([raw[a, t, rows, :] for t in range(4)], axis=1)

    for a in range(3):
        x = jnp.concatenate([by_phase(a, pl.ds(rp, QR, stride=4)) for rp in range(4)], axis=0)
        y = permuted(x, perm[...])
        for rp in range(4):
            for pc in range(4):
                fields[a][rp * 4 + pc, pl.ds(0, QR), pl.ds(0, 128)] = y[rp * QR:(rp + 1) * QR, pc * 128:(pc + 1) * 128]

    def down():
        for pr in range(4):
            for pc in range(4):
                i = pr * 4 + pc
                left = selx[i - 1] if pc > 0 else roll(selx[pr * 4 + 3], 1, 1)
                up = sely[i - 4] if pr > 0 else roll(sely[12 + pc], 1, 0)
                rhs[i] = SCREEN * lum[i] + (left - selx[i]) + (up - sely[i])
        sweep(lum, fa, rhs, w0, 4, 1.0)
        sweep(fa, fb, rhs, w0, 4, 1.0)
        for a in range(2):
            for b in range(2):
                total = None
                for pr in (2 * a, 2 * a + 1):
                    for pc in (2 * b, 2 * b + 1):
                        i = pr * 4 + pc
                        res = (rhs[i] - SCREEN * fb[i]) + (around(fb, pr, pc, 4) - d0[which(pr, pc, 4)] * fb[i])
                        total = res if total is None else total + res
                f1[a * 2 + b] = 0.25 * total
                ea[a * 2 + b] = w1[which(a, b, 2)] * (0.25 * total)
        sweep(ea, eb, f1, w1, 2, 0.5)

    down()
    total = None
    for a in range(2):
        for b in range(2):
            i = a * 2 + b
            res = (f1[i] - SCREEN * eb[i]) + (0.5 * around(eb, a, b, 2) - d1[which(a, b, 2)] * eb[i])
            total = res if total is None else total + res
    total = (0.25 * total) * inside
    turned = jnp.concatenate([total[:, QC:EC], jnp.zeros((128 - ER, 128), F32)], axis=0).T
    strip[r] = jnp.concatenate([total[:, 0:QC], jnp.where(sub8 < 4, turned[0:8], turned[120:128])], axis=0)

    pl.semaphore_wait(barrier, len(peers))

    def send(src, dst, send_sem, recv_sem, device):
        copy = pltpu.make_async_remote_copy(
            src_ref=src, dst_ref=dst, send_sem=send_sem, recv_sem=recv_sem,
            device_id=device, device_id_type=MESH,
        )
        copy.start()
        return copy

    far = [
        send(strip.at[r], strip.at[r], r_send.at[i], r_recv.at[i], (row_peer(d), c)) for i, d in enumerate((4, 2, 6))
    ]
    near = [send(strip.at[r], strip.at[r], r_send.at[3], r_recv.at[3], (sibling, c))]

    lane = lax.broadcasted_iota(jnp.int32, (QR, 128), 1)
    group = lane // 16
    for tile in range(2):
        packed_r = jnp.zeros((QR, 128), F32)
        packed_l = jnp.zeros((QR, 128), F32)
        for g in range(8):
            idx = tile * 8 + g
            if idx >= 12:
                break
            a, rp = divmod(idx, 4)
            edge = raw[a, 3, pl.ds(rp, QR, stride=4), :]
            packed_r = jnp.where(group == g, roll(edge, 16 * g - 112, 1), packed_r)
            edge = raw[a, 0, pl.ds(rp, QR, stride=4), :]
            packed_l = jnp.where(group == g, roll(edge, 16 * g, 1), packed_l)
        to_right[:, pl.ds(tile * 128, 128)] = packed_r
        to_left[:, pl.ds(tile * 128, 128)] = packed_l
    top, bottom = pl.ds(0, 16), pl.ds(H0 - 16, 16)
    body, lo, hi = pl.ds(0, QR), pl.ds(0, 8), pl.ds(QR - 8, 8)
    below, above = pl.ds(QR, 8), pl.ds(QR + 8, 8)
    halo = [
        send(src, dst, h_send.at[i], h_recv.at[i], (row_peer(dr), col_peer(dc)))
        for i, (src, dst, dr, dc) in enumerate([
            (to_right.at[hi], from_l.at[above], 1, 1),
            (to_left.at[hi], from_r.at[above], 1, -1),
            (to_right.at[lo], from_l.at[below], -1, 1),
            (to_left.at[lo], from_r.at[below], -1, -1),
            (to_right, from_l.at[body], 0, 1),
            (to_left, from_r.at[body], 0, -1),
            (raw.at[:, :, bottom], raw.at[:, :, pl.ds(H0 + 16, 16)], 1, 0),
            (raw.at[:, :, top], raw.at[:, :, pl.ds(H0, 16)], -1, 0),
        ])
    ]

    for i, d in ((1, 2), (2, 6), (0, 4)):
        far[i].wait_recv()
        block = row_peer(-d)
        near.append(send(strip.at[block], strip.at[block], r_send.at[4 + i], r_recv.at[4 + i], (sibling, c)))
    for one in consts:
        one.wait()
    for copy in near:
        copy.wait()
    for copy in far:
        copy.wait_send()

    pieces = []
    for o in range(NR):
        first, last = strip[o, pl.ds(0, 8), :], strip[o, pl.ds(QR - 8, 8), :]
        if o > 0:
            first = first + jnp.where(sub8 < 2, strip[o - 1, pl.ds(QR, 8), :], 0.0)
        if o < NR - 1:
            last = last + jnp.where(sub8 >= 6, strip[o + 1, pl.ds(QR, 8), :], 0.0)
        pieces += [first, strip[o, pl.ds(8, QR - 16), :], last]
    whole = jnp.concatenate(pieces, axis=0)
    beside = [strip[o, pl.ds(ER, 8), :] for o in range(NR)]
    pieces = []
    for t in range(4):
        even, odd = beside[2 * t], beside[2 * t + 1]
        x = jnp.where(lane8 < 66, even, 0.0) + jnp.where(lane8 >= 64, roll(odd, 64, 1), 0.0)
        x = x + jnp.where((lane8 >= 62) & (lane8 < 64), roll(odd, -8, 1), 0.0)
        if t < 3:
            x = x + jnp.where(lane8 >= 126, roll(beside[2 * t + 2], 56, 1), 0.0)
        if t > 0:
            x = x + jnp.where(lane8 < 2, roll(beside[2 * t - 1], 64, 1), 0.0)
        pieces.append(x)
    xt = jnp.concatenate([whole.T, jnp.concatenate(pieces, axis=1), jnp.zeros((8, NR * QR), F32)], axis=0)

    xh, xm, xl = split3(xt)
    inner = pl.ds(16, NR * QR)
    ch, cm, cl = ct[0, inner, :], ct[1, inner, :], ct[2, inner, :]
    g = mm(xh, ch) + ((mm(xh, cm) + mm(xm, ch)) + (mm(xm, cm) + (mm(xh, cl) + mm(xl, ch))))
    r1, r2, l2, l1 = (g[QC + i:QC + i + 1] for i in (0, 1, 6, 7))
    g = g[0:QC]

    def small(i):
        return tab[pl.ds(2 * QC + i, 1), :]

    jrow = lax.broadcasted_iota(jnp.int32, (QC, NR * QR), 0)
    fwd, bwd = g, g
    for i, s in enumerate((1, 2, 4, 8, 16, 32, 64)):
        p = small(i)
        fwd = fwd + jnp.where(jrow >= s, roll(fwd, s, 0) * p, 0.0)
        bwd = bwd + jnp.where(jrow < QC - s, roll(bwd, -s, 0) * p, 0.0)
    end, start = fwd[QC - 1:QC], bwd[0:1]
    to_r = end + (small(11) * l1 + small(9) * l2) + (small(12) * r1 + small(13) * r2)
    to_l = start + (small(11) * r1 + small(9) * r2) + (small(12) * l1 + small(13) * l2)
    none = jnp.zeros((1, NR * QR), F32)
    lines = [g[QC - 1:QC], r1, r2, none, to_r, to_l, g[0:1], l1, l2, none]
    mom[c] = jnp.concatenate([x[:, t * 128:(t + 1) * 128] for x in lines for t in range(4)], axis=0)

    copies = []
    for d in range(1, NC):
        part = pl.ds(0, 24) if d == 1 else pl.ds(16, 24) if d == NC - 1 else pl.ds(16, 8)
        copies.append(send(mom.at[c, part], mom.at[c, part], c_send.at[d], c_recv.at[d], (r, col_peer(d))))

    own = small(7) * (fwd + bwd - g)
    near_a = small(7) * (l1 + small(0) * l2)
    near_b = small(7) * (r1 + small(0) * r2)

    for copy in halo:
        copy.wait()
    x = jnp.concatenate([by_phase(a, pl.ds(H0 + rp, 8, stride=4)) for a in range(3) for rp in range(4)], axis=0)
    y = permuted(x, perm[...])
    for a in range(3):
        for rp in range(4):
            i = (a * 4 + rp) * 8
            for pc in range(4):
                fields[a][rp * 4 + pc, pl.ds(QR, 8), pl.ds(0, 128)] = y[i:i + 8, pc * 128:(pc + 1) * 128]
    low8 = sub8 < 4
    lane_e = lax.broadcasted_iota(jnp.int32, (ER, 128), 1)

    def from_side(ref, tile):
        cols = pl.ds(tile * 128, 128)
        return jnp.concatenate(
            [ref[body, cols], jnp.where(low8, ref[below, cols], ref[above, cols])], axis=0
        )

    for a in range(3):
        pieces = []
        for rp in range(4):
            tile, gi = divmod(a * 4 + rp, 8)
            side_l, side_r = from_side(from_l, tile), from_side(from_r, tile)
            pieces.append(jnp.where(lane_e < 64, roll(side_r, -16 * gi, 1), roll(side_l, 112 - 16 * gi, 1)))
        y = permuted(jnp.concatenate(pieces, axis=0), side[...])
        for rp in range(4):
            for pc in range(4):
                fields[a][rp * 4 + pc, :, pl.ds(128, 128)] = y[rp * ER:(rp + 1) * ER, pc * 128:(pc + 1) * 128]
    for i in range(16):
        lum[i] = lum[i] * inside
        if i % 4 == 3:
            selx[i] = selx[i] * inside
        if i // 4 == 3:
            sely[i] = sely[i] * inside
    down()

    for copy in copies:
        copy.wait()

    low = lax.broadcasted_iota(jnp.int32, (8, 128), 0) < 4
    sum_a = jnp.zeros((8, 128), F32)
    sum_b = jnp.zeros((8, 128), F32)
    for o in range(NC):
        m = mom[o, pl.ds(16, 8), :]
        sum_a = sum_a + m * jnp.where(low, dist[lax.rem(c - o + 63, 32)], dist[c + o])
        sum_b = sum_b + m * jnp.where(low, dist[lax.rem(62 - c - o, 32)], dist[lax.rem(o - c + 63, 32)])

    def as_row(x):
        x = x[0:4] + x[4:8]
        return jnp.concatenate([x[t:t + 1] for t in range(4)], axis=1)

    left_m, right_m = mom[col_peer(-1), pl.ds(0, 16), :], mom[col_peer(1), pl.ds(24, 16), :]

    def line(m, i):
        return jnp.concatenate([m[4 * i + t:4 * i + t + 1] for t in range(4)], axis=1)

    a_in, b_in = as_row(sum_a) + near_a, as_row(sum_b) + near_b
    own = own + tab[pl.ds(0, QC), :] * a_in + tab[pl.ds(QC, QC), :] * b_in
    x0 = own[0:1] - 4.0 * line(left_m, 2)
    x127 = own[QC - 1:QC] - 4.0 * line(right_m, 2)
    xs[pl.ds(0, QC), :] = own
    xs[pl.ds(0, 1), :] = x0
    xs[pl.ds(QC - 1, 1), :] = x127
    left1 = a_in + small(8) * start + small(9) * b_in - 4.0 * (line(left_m, 1) + small(10) * line(left_m, 2))
    right1 = b_in + small(8) * end + small(9) * a_in - 4.0 * (line(right_m, 1) + small(10) * line(right_m, 2))
    left2 = small(10) * left1 - x0 - 4.0 * (l1 + line(left_m, 0))
    right2 = small(10) * right1 - x127 - 4.0 * (r1 + line(right_m, 0))
    zero6 = jnp.zeros((6, NR * QR), F32)
    xs[pl.ds(QC, 8), :] = jnp.concatenate([right1, right2, zero6], axis=0)
    xs[pl.ds(EC - 8, 8), :] = jnp.concatenate([zero6, left2, left1], axis=0)

    base = pl.multiple_of(r * QR, QR)
    sub16 = lax.broadcasted_iota(jnp.int32, (16, NR * QR), 0)
    back = []
    for i in range(3):
        tail = jnp.where(
            sub16 < 8,
            ct[i, pl.ds(base + QR + 16, 16), :].astype(F32),
            ct[i, pl.ds(base, 16), :].astype(F32),
        ).astype(BF)
        back.append(jnp.concatenate([ct[i, pl.ds(base + 16, QR), :], tail], axis=0))
    th, tm, tl = back
    xh, xm, xl = split3(xs[...])
    nt = ((1,), (1,))
    e2 = mm(th, xh, nt) + ((mm(th, xm, nt) + mm(tm, xh, nt)) + (mm(tm, xm, nt) + (mm(th, xl, nt) + mm(tl, xh, nt))))
    sub8 = lax.broadcasted_iota(jnp.int32, (8, EC), 0)
    e2 = jnp.concatenate([e2[0:QR], jnp.where(sub8 < 4, e2[QR:QR + 8], e2[QR + 8:QR + 16])], axis=0)
    e2 = e2 * inside

    for i in range(4):
        ea[i] = eb[i] + e2
    sweep(ea, ec, f1, w1, 2, 0.5)
    sweep(ec, ea, f1, w1, 2, 0.5)
    for pr in range(4):
        for pc in range(4):
            fa[pr * 4 + pc] = fb[pr * 4 + pc] + ea[(pr // 2) * 2 + pc // 2]
    sweep(fa, lum, rhs, w0, 4, 1.0)
    sweep(lum, fb, rhs, w0, 4, 1.0)
    x = jnp.concatenate([
        jnp.concatenate([fb[pr * 4 + pc, pl.ds(0, QR), pl.ds(0, QC)] for pc in range(4)], axis=1)
        for pr in range(4)
    ], axis=0)
    y = permuted(x, permt[...])
    for pr in range(4):
        for t in range(4):
            out[t, pl.ds(pr, QR, stride=4), :] = y[pr * QR:(pr + 1) * QR, t * 128:(t + 1) * 128]
    copies = [
        pltpu.make_async_copy(out.at[t], out_h.at[:, pl.ds(t * 128, 128)], out_sem.at[t]) for t in range(4)
    ]
    for copy in copies:
        copy.start()
    for copy in copies:
        copy.wait()


def shards(luminance, grad_x, grad_y, labels):
    consts = tables()
    vmem = pltpu.VMEM
    phases = vmem((16, ER, EC), F32)
    quarter = vmem((4, ER, EC), F32)
    nine = vmem((9, ER, EC), F32)
    dma = pltpu.SemaphoreType.DMA
    return pl.pallas_call(
        kernel,
        out_shape=jax.ShapeDtypeStruct((H0, W0), F32),
        in_specs=[pl.BlockSpec(memory_space=pl.ANY)] * 7,
        out_specs=pl.BlockSpec(memory_space=pl.ANY),
        scratch_shapes=[
            vmem((4, H0, W0), F32),
            vmem((4, H0, W0), F32),
            vmem((H0, W0), jnp.int32),
            vmem((3, 4, H0 + 32, 128), F32),
            vmem((W0, W0), BF),
            vmem((W0, W0), BF),
            vmem((128, W0), BF),
            vmem(consts[0].shape, BF),
            vmem(consts[1].shape, F32),
            vmem(consts[2].shape, F32),
            vmem((QR, 256), F32),
            vmem((QR, 256), F32),
            vmem((QR + 16, 256), F32),
            vmem((QR + 16, 256), F32),
            phases, phases, phases, phases, phases, phases,
            nine, nine, nine, nine,
            quarter, quarter, quarter, quarter,
            vmem((NR, ER + 8, QC), F32),
            vmem((NC, 40, 128), F32),
            vmem((EC, NR * QR), F32),
            vmem((4, H0, 128), F32),
            dma((4, 7)),
            dma((3,)),
            dma((4,)),
            dma((8,)),
            dma((8,)),
            dma((NR,)),
            dma((NR,)),
            dma((NC,)),
            dma((NC,)),
        ],
        compiler_params=pltpu.CompilerParams(
            collective_id=0, has_side_effects=True, vmem_limit_bytes=56 * 1024 * 1024
        ),
    )(luminance, grad_x, grad_y, labels, *[jnp.asarray(x) for x in consts])


def solution(mesh):
    return jax.shard_map(
        shards,
        mesh=mesh,
        in_specs=(
            P("rows", "cols"),
            P(None, "rows", "cols"),
            P(None, "rows", "cols"),
            P("rows", "cols"),
        ),
        out_specs=P("rows", "cols"),
        check_vma=False,
    )
```

time: 33.7 us -> 28.4 us (0.84)
  Pallas kernels: 31.6 us -> 26.4 us
    pallas_call x1, Pallas kernels: 31.6 us -> 26.4 us  [shards(): pl.pallas_call(kernel, out_shape=jax.ShapeDtypeStruct((H0, W0), F32), in_...]
where the time goes in v2:
time: 28.4 us; the launch traced here: 28.2 us
  Pallas kernels  26.4 us (93%)
  local copies, waits for them, and re-layouts  1.87 us (7%)
    pallas_call x1, Pallas kernels, shards(): pl.pallas_call(kernel, out_shape=jax.ShapeDtypeStruct((H0, W0), F32), in_...  26.4 us
    unnamed x1, local copies, waits for them, and re-layouts  1.87 us

profile of v2, /device:TPU:1, one launch (start us, length us, event | category | flops | bytes accessed | tf_op | source)
XLA Modules:
  0.0 28.2 jit_solution(15236101833307263183)
XLA Ops:
  0.0 26.4 %shard_map.73 = f32[256,512]{1,0:T(8,128)} custom-call(f32[256,512]{1,0:T(8,128)} %lum_h.1, f32[4,256,512]{2,1,0:T(8,128)} %gx_h.1, f32[4,256,512]{2,1,0:T(8,128)} %gy_h.1, s32[256,512]{1,0:T(8,128)} %lab_h.1, bf16[3,544,512]{2,1,0:T(8,128)(2,1)} %constant.6.clone.ct_h, f32[272,512]{1,0:T(8,128)} %constant.7.clone.tab_h, f32[32,8,128]{2,1,0:T(8,128)} %constant.8.clone.dist_h), custom_call_target="tpu_custom_call" | custom-call | tf_op jit(solution)/shard_map/pallas_call | solution.py:510
  26.4 1.9 %copy.9 = f32[256,512]{1,0:T(8,128)} copy(f32[256,512]{1,0:T(8,128)} %shard_map.73) | data formatting | bytes 1048576

commit v3 on v2

--- a/solution.py
+++ b/solution.py
@@ -39,6 +39,8 @@
     scale = np.where(k == 0, math.sqrt(1.0 / rows), math.sqrt(2.0 / rows))
     ct = np.zeros((rows + 32, rows))
     ct[16:-16] = scale[None, :] * np.cos(phase * (math.pi / (2 * rows)))
+    ct[:16] = ct[31:15:-1]
+    ct[-16:] = ct[-17:-33:-1]
     ct = np.stack(bf16_parts(ct, 3))
     mu = SCREEN + 0.25 * 4 * np.sin(np.pi * k / (2 * rows)) ** 2
     half = 1 + 2 * mu
@@ -114,14 +116,20 @@
             dst[i] = (1 - OMEGA) * src[i] + w[which(pr, pc, n)] * (f[i] + nb)
 
 
+def distance(d):
+    ring = (0, 1, 2, 1, 0)
+    dy, dz = divmod(d, 4)
+    return ring[dz] + ((4 - dz) * ring[dy] + dz * ring[dy + 1]) / 4
+
+
 def kernel(
     lum_h, gx_h, gy_h, lab_h, ct_h, tab_h, dist_h,
     out_h,
     gx, gy, lab, raw, perm, permt, side, ct, tab, dist,
     to_right, to_left, from_l, from_r,
     lum, selx, sely, rhs, fa, fb, w0, d0, w1, d1, f1, ea, eb, ec,
-    strip, mom, xs, out,
-    in_sem, const_sem, out_sem, h_send, h_recv, r_send, r_recv, c_send, c_recv,
+    strip, share_m, mom, out,
+    in_sem, const_sem, out_sem, h_send, h_recv, r_send, r_recv, m_send, m_recv, c_send, c_recv,
 ):
     r = lax.axis_index("rows")
     c = lax.axis_index("cols")
@@ -134,8 +142,9 @@
 
     sibling = r + 1 - 2 * lax.rem(r, 2)
     barrier = pltpu.get_barrier_semaphore()
-    peers = [(d, 0) for d in (1, 2, 4, 6, 7)] + [(0, d) for d in range(1, NC)]
-    peers += [(1, 1), (1, -1), (-1, 1), (-1, -1)]
+    row_order = (4, 3, 5, 2, 6, 1, 7)
+    col_order = sorted(range(1, NC), key=lambda d: -distance(d))
+    peers = [(0, d) for d in col_order] + [(1, 1), (1, -1), (-1, 1), (-1, -1)] + [(d, 0) for d in row_order]
     for dr, dc in peers:
         pl.semaphore_signal(
             barrier, inc=1, device_id=(row_peer(dr), col_peer(dc)), device_id_type=MESH
@@ -193,7 +202,6 @@
                     continue
                 dr_[3 * a + b] = coef * deg
                 wr[3 * a + b] = inside * (OMEGA / (SCREEN + coef * deg))
-    xs[...] = jnp.zeros_like(xs)
     fields = (lum, selx, sely)
     for field in fields:
         for i in range(16):
@@ -261,16 +269,61 @@
                 ea[a * 2 + b] = w1[which(a, b, 2)] * (0.25 * total)
         sweep(ea, eb, f1, w1, 2, 0.5)
 
+    def coarsest():
+        total = None
+        for a in range(2):
+            for b in range(2):
+                i = a * 2 + b
+                res = (f1[i] - SCREEN * eb[i]) + (0.5 * around(eb, a, b, 2) - d1[which(a, b, 2)] * eb[i])
+                total = res if total is None else total + res
+        return 0.25 * total
+
     down()
-    total = None
-    for a in range(2):
-        for b in range(2):
-            i = a * 2 + b
-            res = (f1[i] - SCREEN * eb[i]) + (0.5 * around(eb, a, b, 2) - d1[which(a, b, 2)] * eb[i])
-            total = res if total is None else total + res
-    total = (0.25 * total) * inside
-    turned = jnp.concatenate([total[:, QC:EC], jnp.zeros((128 - ER, 128), F32)], axis=0).T
-    strip[r] = jnp.concatenate([total[:, 0:QC], jnp.where(sub8 < 4, turned[0:8], turned[120:128])], axis=0)
+    total = coarsest() * inside
+    tail = total[QR:ER]
+    tall = jnp.concatenate([
+        total[0:QR],
+        jnp.where(sub8[:, :1] < 4, tail, 0.0), jnp.where(sub8[:, :1] >= 4, tail, 0.0),
+        jnp.zeros((48, EC), F32),
+    ], axis=0)
+    turned = tall[:, QC:EC].T
+    beside = jnp.where(sub8 < 4, turned[0:8], turned[120:128])
+    strip[r] = jnp.concatenate([total[:, 0:QC], beside], axis=0)
+    own_t = jnp.concatenate([tall[:, 0:QC].T, beside, jnp.zeros((8, 128), F32)], axis=0)
+    for one in consts:
+        one.wait()
+
+    def small(i):
+        return tab[pl.ds(2 * QC + i, 1), :]
+
+    def six(xs_, cs_, dims=((1,), (0,))):
+        (xh, xm, xl), (ch, cm, cl) = xs_, cs_
+        return mm(xh, ch, dims) + (
+            (mm(xh, cm, dims) + mm(xm, ch, dims)) + (mm(xm, cm, dims) + (mm(xh, cl, dims) + mm(xl, ch, dims)))
+        )
+
+    base = pl.multiple_of(r * QR, QR)
+    sub16 = lax.broadcasted_iota(jnp.int32, (16, NR * QR), 0)
+    back = []
+    for i in range(3):
+        tail = jnp.where(
+            sub16 < 8,
+            ct[i, pl.ds(base + QR + 16, 16), :].astype(F32),
+            ct[i, pl.ds(base, 16), :].astype(F32),
+        ).astype(BF)
+        back.append(jnp.concatenate([ct[i, pl.ds(base + 16, QR), :], tail], axis=0))
+    pad = jnp.zeros((48, NR * QR), BF)
+    share = six(split3(own_t), [jnp.concatenate([x, pad], axis=0) for x in back])
+    r1, r2, l2, l1 = (share[QC + i:QC + i + 1] for i in (0, 1, 6, 7))
+    share = share[0:QC]
+    to_r = jnp.sum(share * tab[pl.ds(QC, QC), :], axis=0, keepdims=True)
+    to_l = jnp.sum(share * tab[pl.ds(0, QC), :], axis=0, keepdims=True)
+    to_r = small(12) * (to_r + r1 + small(12) * r2) + (small(11) * l1 + small(9) * l2)
+    to_l = small(12) * (to_l + l1 + small(12) * l2) + (small(11) * r1 + small(9) * r2)
+    def in_rows(xs_):
+        return jnp.concatenate([x[:, t * 128:(t + 1) * 128] for x in xs_ for t in range(4)], axis=0)
+
+    share_m[r] = in_rows([to_r, to_l, r2, l2])
 
     pl.semaphore_wait(barrier, len(peers))
 
@@ -281,6 +334,8 @@
         )
         copy.start()
         return copy
+
+    copies = [send(share_m.at[r], share_m.at[r], m_send.at[d], m_recv.at[d], (row_peer(d), c)) for d in row_order]
 
     far = [
         send(strip.at[r], strip.at[r], r_send.at[i], r_recv.at[i], (row_peer(d), c)) for i, d in enumerate((4, 2, 6))
@@ -320,12 +375,19 @@
         ])
     ]
 
+    for copy in copies:
+        copy.wait()
+    m = share_m[...]
+    mom[c] = ((m[0] + m[1]) + (m[2] + m[3])) + ((m[4] + m[5]) + (m[6] + m[7]))
+    copies = []
+    for d in col_order:
+        block = mom.at[c, pl.ds(0, 16 if d in (1, NC - 1) else 8)]
+        copies.append(send(block, block, c_send.at[d], c_recv.at[d], (r, col_peer(d))))
+
     for i, d in ((1, 2), (2, 6), (0, 4)):
         far[i].wait_recv()
         block = row_peer(-d)
         near.append(send(strip.at[block], strip.at[block], r_send.at[4 + i], r_recv.at[4 + i], (sibling, c)))
-    for one in consts:
-        one.wait()
     for copy in near:
         copy.wait()
     for copy in far:
@@ -345,23 +407,18 @@
     for t in range(4):
         even, odd = beside[2 * t], beside[2 * t + 1]
         x = jnp.where(lane8 < 66, even, 0.0) + jnp.where(lane8 >= 64, roll(odd, 64, 1), 0.0)
-        x = x + jnp.where((lane8 >= 62) & (lane8 < 64), roll(odd, -8, 1), 0.0)
+        x = x + jnp.where((lane8 >= 62) & (lane8 < 64), roll(odd, -16, 1), 0.0)
         if t < 3:
-            x = x + jnp.where(lane8 >= 126, roll(beside[2 * t + 2], 56, 1), 0.0)
+            x = x + jnp.where(lane8 >= 126, roll(beside[2 * t + 2], 48, 1), 0.0)
         if t > 0:
             x = x + jnp.where(lane8 < 2, roll(beside[2 * t - 1], 64, 1), 0.0)
         pieces.append(x)
     xt = jnp.concatenate([whole.T, jnp.concatenate(pieces, axis=1), jnp.zeros((8, NR * QR), F32)], axis=0)
 
-    xh, xm, xl = split3(xt)
     inner = pl.ds(16, NR * QR)
-    ch, cm, cl = ct[0, inner, :], ct[1, inner, :], ct[2, inner, :]
-    g = mm(xh, ch) + ((mm(xh, cm) + mm(xm, ch)) + (mm(xm, cm) + (mm(xh, cl) + mm(xl, ch))))
+    g = six(split3(xt), [ct[i, inner, :] for i in range(3)])
     r1, r2, l2, l1 = (g[QC + i:QC + i + 1] for i in (0, 1, 6, 7))
     g = g[0:QC]
-
-    def small(i):
-        return tab[pl.ds(2 * QC + i, 1), :]
 
     jrow = lax.broadcasted_iota(jnp.int32, (QC, NR * QR), 0)
     fwd, bwd = g, g
@@ -370,21 +427,9 @@
         fwd = fwd + jnp.where(jrow >= s, roll(fwd, s, 0) * p, 0.0)
         bwd = bwd + jnp.where(jrow < QC - s, roll(bwd, -s, 0) * p, 0.0)
     end, start = fwd[QC - 1:QC], bwd[0:1]
-    to_r = end + (small(11) * l1 + small(9) * l2) + (small(12) * r1 + small(13) * r2)
-    to_l = start + (small(11) * r1 + small(9) * r2) + (small(12) * l1 + small(13) * l2)
-    none = jnp.zeros((1, NR * QR), F32)
-    lines = [g[QC - 1:QC], r1, r2, none, to_r, to_l, g[0:1], l1, l2, none]
-    mom[c] = jnp.concatenate([x[:, t * 128:(t + 1) * 128] for x in lines for t in range(4)], axis=0)
-
-    copies = []
-    for d in range(1, NC):
-        part = pl.ds(0, 24) if d == 1 else pl.ds(16, 24) if d == NC - 1 else pl.ds(16, 8)
-        copies.append(send(mom.at[c, part], mom.at[c, part], c_send.at[d], c_recv.at[d], (r, col_peer(d))))
-
     own = small(7) * (fwd + bwd - g)
     near_a = small(7) * (l1 + small(0) * l2)
     near_b = small(7) * (r1 + small(0) * r2)
-
     for copy in halo:
         copy.wait()
     x = jnp.concatenate([by_phase(a, pl.ds(H0 + rp, 8, stride=4)) for a in range(3) for rp in range(4)], axis=0)
@@ -420,56 +465,47 @@
         if i // 4 == 3:
             sely[i] = sely[i] * inside
     down()
+    f2 = coarsest()
+    f2 = jnp.concatenate([f2, f2[QR:ER]], axis=0)
 
     for copy in copies:
         copy.wait()
-
-    low = lax.broadcasted_iota(jnp.int32, (8, 128), 0) < 4
+    low = sub8 < 4
     sum_a = jnp.zeros((8, 128), F32)
     sum_b = jnp.zeros((8, 128), F32)
     for o in range(NC):
-        m = mom[o, pl.ds(16, 8), :]
+        m = mom[o, pl.ds(0, 8), :]
         sum_a = sum_a + m * jnp.where(low, dist[lax.rem(c - o + 63, 32)], dist[c + o])
         sum_b = sum_b + m * jnp.where(low, dist[lax.rem(62 - c - o, 32)], dist[lax.rem(o - c + 63, 32)])
 
-    def as_row(x):
-        x = x[0:4] + x[4:8]
-        return jnp.concatenate([x[t:t + 1] for t in range(4)], axis=1)
-
-    left_m, right_m = mom[col_peer(-1), pl.ds(0, 16), :], mom[col_peer(1), pl.ds(24, 16), :]
-
     def line(m, i):
         return jnp.concatenate([m[4 * i + t:4 * i + t + 1] for t in range(4)], axis=1)
 
-    a_in, b_in = as_row(sum_a) + near_a, as_row(sum_b) + near_b
+    a_in = line(sum_a[0:4] + sum_a[4:8], 0) + near_a
+    b_in = line(sum_b[0:4] + sum_b[4:8], 0) + near_b
     own = own + tab[pl.ds(0, QC), :] * a_in + tab[pl.ds(QC, QC), :] * b_in
-    x0 = own[0:1] - 4.0 * line(left_m, 2)
-    x127 = own[QC - 1:QC] - 4.0 * line(right_m, 2)
-    xs[pl.ds(0, QC), :] = own
-    xs[pl.ds(0, 1), :] = x0
-    xs[pl.ds(QC - 1, 1), :] = x127
-    left1 = a_in + small(8) * start + small(9) * b_in - 4.0 * (line(left_m, 1) + small(10) * line(left_m, 2))
-    right1 = b_in + small(8) * end + small(9) * a_in - 4.0 * (line(right_m, 1) + small(10) * line(right_m, 2))
-    left2 = small(10) * left1 - x0 - 4.0 * (l1 + line(left_m, 0))
-    right2 = small(10) * right1 - x127 - 4.0 * (r1 + line(right_m, 0))
-    zero6 = jnp.zeros((6, NR * QR), F32)
-    xs[pl.ds(QC, 8), :] = jnp.concatenate([right1, right2, zero6], axis=0)
-    xs[pl.ds(EC - 8, 8), :] = jnp.concatenate([zero6, left2, left1], axis=0)
-
-    base = pl.multiple_of(r * QR, QR)
-    sub16 = lax.broadcasted_iota(jnp.int32, (16, NR * QR), 0)
-    back = []
-    for i in range(3):
-        tail = jnp.where(
-            sub16 < 8,
-            ct[i, pl.ds(base + QR + 16, 16), :].astype(F32),
-            ct[i, pl.ds(base, 16), :].astype(F32),
-        ).astype(BF)
-        back.append(jnp.concatenate([ct[i, pl.ds(base + 16, QR), :], tail], axis=0))
-    th, tm, tl = back
-    xh, xm, xl = split3(xs[...])
-    nt = ((1,), (1,))
-    e2 = mm(th, xh, nt) + ((mm(th, xm, nt) + mm(tm, xh, nt)) + (mm(tm, xm, nt) + (mm(th, xl, nt) + mm(tl, xh, nt))))
+    own = own - 4.0 * jnp.concatenate([
+        line(mom[col_peer(-1), pl.ds(8, 8), :], 0), jnp.zeros((QC - 2, NR * QR), F32),
+        line(mom[col_peer(1), pl.ds(8, 8), :], 1),
+    ], axis=0)
+
+    e2 = six(back, split3(own), ((1,), (1,)))
+
+    lane = lax.broadcasted_iota(jnp.int32, (ER + 8, 128), 1)
+
+    row = lax.broadcasted_iota(jnp.int32, (ER + 8, 128), 0)
+
+    def beyond(inner, at, f):
+        up = jnp.where((r == 0) & (row == 0), at, roll(at, 1, 0))
+        down = jnp.where((r == NR - 1) & (row == QR - 1), at, roll(at, -1, 0))
+        return 4.0 * ((1 + SCREEN) * at - f) - (up + down) - inner
+
+    one = beyond(jnp.where(lane < 64, roll(e2, -1, 1), roll(e2, 1, 1)), e2, f2[:, 0:QC])
+    side_f = f2[:, QC:EC]
+    two = beyond(e2, one, jnp.where(lane < 64, roll(side_f, 1, 1), roll(side_f, -1, 1)))
+    outer = jnp.where(lane == 0, roll(one, 1, 1), jnp.where(lane == 1, roll(two, 2, 1), 0.0))
+    outer = jnp.where(lane == 127, roll(one, -1, 1), jnp.where(lane == 126, roll(two, -2, 1), outer))
+    e2 = jnp.concatenate([e2, outer], axis=1)
     sub8 = lax.broadcasted_iota(jnp.int32, (8, EC), 0)
     e2 = jnp.concatenate([e2[0:QR], jnp.where(sub8 < 4, e2[QR:QR + 8], e2[QR + 8:QR + 16])], axis=0)
     e2 = e2 * inside
@@ -531,14 +567,16 @@
             nine, nine, nine, nine,
             quarter, quarter, quarter, quarter,
             vmem((NR, ER + 8, QC), F32),
-            vmem((NC, 40, 128), F32),
-            vmem((EC, NR * QR), F32),
+            vmem((NR, 16, 128), F32),
+            vmem((NC, 16, 128), F32),
             vmem((4, H0, 128), F32),
             dma((4, 7)),
             dma((3,)),
             dma((4,)),
             dma((8,)),
             dma((8,)),
+            dma((NR,)),
+            dma((NR,)),
             dma((NR,)),
             dma((NR,)),
             dma((NC,)),

time: 28.4 us -> 25.8 us (0.908)
  Pallas kernels: 26.4 us -> 23.8 us
    pallas_call x1, Pallas kernels: 26.4 us -> 23.8 us  [shards(): pl.pallas_call(kernel, out_shape=jax.ShapeDtypeStruct((H0, W0), F32), in_...]
where the time goes in v3:
time: 25.8 us; the launch traced here: 25.6 us
  Pallas kernels  23.8 us (92%)
  local copies, waits for them, and re-layouts  1.87 us (7%)
    pallas_call x1, Pallas kernels, shards(): pl.pallas_call(kernel, out_shape=jax.ShapeDtypeStruct((H0, W0), F32), in_...  23.8 us
    unnamed x1, local copies, waits for them, and re-layouts  1.87 us

profile of v3, /device:TPU:1, one launch (start us, length us, event | category | flops | bytes accessed | tf_op | source)
XLA Modules:
  0.0 25.6 jit_solution(6143353969557299950)
XLA Ops:
  0.0 23.8 %shard_map.73 = f32[256,512]{1,0:T(8,128)} custom-call(f32[256,512]{1,0:T(8,128)} %lum_h.1, f32[4,256,512]{2,1,0:T(8,128)} %gx_h.1, f32[4,256,512]{2,1,0:T(8,128)} %gy_h.1, s32[256,512]{1,0:T(8,128)} %lab_h.1, bf16[3,544,512]{2,1,0:T(8,128)(2,1)} %constant.6.clone.ct_h, f32[272,512]{1,0:T(8,128)} %constant.7.clone.tab_h, f32[32,8,128]{2,1,0:T(8,128)} %constant.8.clone.dist_h), custom_call_target="tpu_custom_call" | custom-call | tf_op jit(solution)/shard_map/pallas_call | solution.py:546
  23.8 1.9 %copy.9 = f32[256,512]{1,0:T(8,128)} copy(f32[256,512]{1,0:T(8,128)} %shard_map.73) | data formatting | bytes 1048576

commit v4 on v3

--- a/solution.py
+++ b/solution.py
@@ -158,13 +158,13 @@
             pltpu.make_async_copy(gx_h.at[:, rows], gx.at[:, rows], in_sem.at[i, 0]),
             pltpu.make_async_copy(gy_h.at[:, rows], gy.at[:, rows], in_sem.at[i, 1]),
             pltpu.make_async_copy(lab_h.at[rows], lab.at[rows], in_sem.at[i, 2]),
-        ] + [
-            pltpu.make_async_copy(lum_h.at[rows, pl.ds(t * 128, 128)], raw.at[0, t, rows], in_sem.at[i, 3 + t])
-            for t in range(4)
         ])
-    for group in loads:
-        for one in group:
-            one.start()
+    lum_loads = [
+        pltpu.make_async_copy(lum_h.at[:, pl.ds(t * 128, 128)], raw.at[0, t, pl.ds(0, H0)], in_sem.at[t, 3])
+        for t in range(4)
+    ]
+    for one in lum_loads + [one for group in loads for one in group]:
+        one.start()
     consts = [
         pltpu.make_async_copy(a, b, const_sem.at[i])
         for i, (a, b) in enumerate([(ct_h, ct), (tab_h, tab), (dist_h, dist)])
@@ -208,6 +208,20 @@
             field[i, pl.ds(QR, 8), pl.ds(0, QC)] = jnp.zeros((8, QC), F32)
             field[i, :, pl.ds(QC, 128)] = jnp.zeros((ER, 128), F32)
 
+    def by_phase(a, rows):
+        return jnp.concatenate([raw[a, t, rows, :] for t in range(4)], axis=1)
+
+    def own_by_phase(a):
+        x = jnp.concatenate([by_phase(a, pl.ds(rp, QR, stride=4)) for rp in range(4)], axis=0)
+        y = permuted(x, perm[...])
+        for rp in range(4):
+            for pc in range(4):
+                fields[a][rp * 4 + pc, pl.ds(0, QR), pl.ds(0, 128)] = y[rp * QR:(rp + 1) * QR, pc * 128:(pc + 1) * 128]
+
+    for one in lum_loads:
+        one.wait()
+    own_by_phase(0)
+
     lane8 = lax.broadcasted_iota(jnp.int32, (8, 128), 1)
     sub8 = lax.broadcasted_iota(jnp.int32, (8, 128), 0)
     for i in range(H0 // CH):
@@ -238,15 +252,8 @@
     for one in consts:
         one.start()
 
-    def by_phase(a, rows):
-        return jnp.concatenate([raw[a, t, rows, :] for t in range(4)], axis=1)
-
-    for a in range(3):
-        x = jnp.concatenate([by_phase(a, pl.ds(rp, QR, stride=4)) for rp in range(4)], axis=0)
-        y = permuted(x, perm[...])
-        for rp in range(4):
-            for pc in range(4):
-                fields[a][rp * 4 + pc, pl.ds(0, QR), pl.ds(0, 128)] = y[rp * QR:(rp + 1) * QR, pc * 128:(pc + 1) * 128]
+    own_by_phase(1)
+    own_by_phase(2)
 
     def down():
         for pr in range(4):
@@ -570,7 +577,7 @@
             vmem((NR, 16, 128), F32),
             vmem((NC, 16, 128), F32),
             vmem((4, H0, 128), F32),
-            dma((4, 7)),
+            dma((4, 4)),
             dma((3,)),
             dma((4,)),
             dma((8,)),

time: 25.8 us -> 25.5 us (0.988)
  Pallas kernels: 23.8 us -> 23.5 us
where the time goes in v4:
time: 25.5 us; the launch traced here: 25.4 us
  Pallas kernels  23.5 us (92%)
  local copies, waits for them, and re-layouts  1.87 us (7%)
    pallas_call x1, Pallas kernels, shards(): pl.pallas_call(kernel, out_shape=jax.ShapeDtypeStruct((H0, W0), F32), in_...  23.5 us
    unnamed x1, local copies, waits for them, and re-layouts  1.87 us

profile of v4, /device:TPU:1, one launch (start us, length us, event | category | flops | bytes accessed | tf_op | source)
XLA Modules:
  0.0 25.4 jit_solution(485746631164205409)
XLA Ops:
  0.0 23.5 %shard_map.73 = f32[256,512]{1,0:T(8,128)} custom-call(f32[256,512]{1,0:T(8,128)} %lum_h.1, f32[4,256,512]{2,1,0:T(8,128)} %gx_h.1, f32[4,256,512]{2,1,0:T(8,128)} %gy_h.1, s32[256,512]{1,0:T(8,128)} %lab_h.1, bf16[3,544,512]{2,1,0:T(8,128)(2,1)} %constant.6.clone.ct_h, f32[272,512]{1,0:T(8,128)} %constant.7.clone.tab_h, f32[32,8,128]{2,1,0:T(8,128)} %constant.8.clone.dist_h), custom_call_target="tpu_custom_call" | custom-call | tf_op jit(solution)/shard_map/pallas_call | solution.py:553
  23.5 1.9 %copy.9 = f32[256,512]{1,0:T(8,128)} copy(f32[256,512]{1,0:T(8,128)} %shard_map.73) | data formatting | bytes 1048576

commit v5 on v4

--- a/solution.py
+++ b/solution.py
@@ -122,6 +122,23 @@
     return ring[dz] + ((4 - dz) * ring[dy] + dz * ring[dy + 1]) / 4
 
 
+def last_sweep(src, dst, f, w):
+    own = (pl.ds(0, QR), pl.ds(0, QC))
+
+    def rolled(i, shift, axis):
+        return roll(src[i], shift, axis)[0:QR, 0:QC]
+
+    for pr in range(4):
+        for pc in range(4):
+            i = pr * 4 + pc
+            up = src[(i - 4, *own)] if pr > 0 else rolled(12 + pc, 1, 0)
+            down = src[(i + 4, *own)] if pr < 3 else rolled(pc, -1, 0)
+            left = src[(i - 1, *own)] if pc > 0 else rolled(i + 3, 1, 1)
+            right = src[(i + 1, *own)] if pc < 3 else rolled(i - 3, -1, 1)
+            nb = (up + down) + (left + right)
+            dst[(i, *own)] = (1 - OMEGA) * src[(i, *own)] + w[(which(pr, pc, 4), *own)] * (f[(i, *own)] + nb)
+
+
 def kernel(
     lum_h, gx_h, gy_h, lab_h, ct_h, tab_h, dist_h,
     out_h,
@@ -525,20 +542,23 @@
         for pc in range(4):
             fa[pr * 4 + pc] = fb[pr * 4 + pc] + ea[(pr // 2) * 2 + pc // 2]
     sweep(fa, lum, rhs, w0, 4, 1.0)
-    sweep(lum, fb, rhs, w0, 4, 1.0)
-    x = jnp.concatenate([
-        jnp.concatenate([fb[pr * 4 + pc, pl.ds(0, QR), pl.ds(0, QC)] for pc in range(4)], axis=1)
-        for pr in range(4)
-    ], axis=0)
-    y = permuted(x, permt[...])
-    for pr in range(4):
+    last_sweep(lum, fb, rhs, w0)
+    copies = []
+    half = QR // 2
+    for h in range(2):
+        x = jnp.concatenate([
+            jnp.concatenate([fb[pr * 4 + pc, pl.ds(h * half, half), pl.ds(0, QC)] for pc in range(4)], axis=1)
+            for pr in range(4)
+        ], axis=0)
+        y = permuted(x, permt[...])
+        rows = pl.ds(h * 4 * half, 4 * half)
+        for pr in range(4):
+            for t in range(4):
+                out[t, pl.ds(h * 4 * half + pr, half, stride=4), :] = y[pr * half:(pr + 1) * half, t * 128:(t + 1) * 128]
         for t in range(4):
-            out[t, pl.ds(pr, QR, stride=4), :] = y[pr * QR:(pr + 1) * QR, t * 128:(t + 1) * 128]
-    copies = [
-        pltpu.make_async_copy(out.at[t], out_h.at[:, pl.ds(t * 128, 128)], out_sem.at[t]) for t in range(4)
-    ]
-    for copy in copies:
-        copy.start()
+            copy = pltpu.make_async_copy(out.at[t, rows], out_h.at[rows, pl.ds(t * 128, 128)], out_sem.at[h, t])
+            copy.start()
+            copies.append(copy)
     for copy in copies:
         copy.wait()
 
@@ -579,7 +599,7 @@
             vmem((4, H0, 128), F32),
             dma((4, 4)),
             dma((3,)),
-            dma((4,)),
+            dma((2, 4)),
             dma((8,)),
             dma((8,)),
             dma((NR,)),

time: 25.5 us -> 25.5 us (level)
  no operation moved by 1% of the time
where the time goes in v5:
time: 25.5 us; the launch traced here: 25.3 us
  Pallas kernels  23.4 us (92%)
  local copies, waits for them, and re-layouts  1.87 us (7%)
    pallas_call x1, Pallas kernels, shards(): pl.pallas_call(kernel, out_shape=jax.ShapeDtypeStruct((H0, W0), F32), in_...  23.4 us
    unnamed x1, local copies, waits for them, and re-layouts  1.87 us

profile of v5, /device:TPU:1, one launch (start us, length us, event | category | flops | bytes accessed | tf_op | source)
XLA Modules:
  0.0 25.3 jit_solution(8169742578611272488)
XLA Ops:
  0.0 23.4 %shard_map.73 = f32[256,512]{1,0:T(8,128)} custom-call(f32[256,512]{1,0:T(8,128)} %lum_h.1, f32[4,256,512]{2,1,0:T(8,128)} %gx_h.1, f32[4,256,512]{2,1,0:T(8,128)} %gy_h.1, s32[256,512]{1,0:T(8,128)} %lab_h.1, bf16[3,544,512]{2,1,0:T(8,128)(2,1)} %constant.6.clone.ct_h, f32[272,512]{1,0:T(8,128)} %constant.7.clone.tab_h, f32[32,8,128]{2,1,0:T(8,128)} %constant.8.clone.dist_h), custom_call_target="tpu_custom_call" | custom-call | tf_op jit(solution)/shard_map/pallas_call | solution.py:573
  23.4 1.9 %copy.9 = f32[256,512]{1,0:T(8,128)} copy(f32[256,512]{1,0:T(8,128)} %shard_map.73) | data formatting | bytes 1048576

commit v6 on v4

--- a/solution.py
+++ b/solution.py
@@ -126,7 +126,7 @@
     lum_h, gx_h, gy_h, lab_h, ct_h, tab_h, dist_h,
     out_h,
     gx, gy, lab, raw, perm, permt, side, ct, tab, dist,
-    to_right, to_left, from_l, from_r,
+    to_right, to_left, from_l, from_r, fold_r, fold_l, fold_from_l, fold_from_r,
     lum, selx, sely, rhs, fa, fb, w0, d0, w1, d1, f1, ea, eb, ec,
     strip, share_m, mom, out,
     in_sem, const_sem, out_sem, h_send, h_recv, r_send, r_recv, m_send, m_recv, c_send, c_recv,
@@ -365,6 +365,9 @@
             packed_l = jnp.where(group == g, roll(edge, 16 * g, 1), packed_l)
         to_right[:, pl.ds(tile * 128, 128)] = packed_r
         to_left[:, pl.ds(tile * 128, 128)] = packed_l
+    half = QR // 2
+    fold_r[...] = jnp.where(lane[0:half] < 64, packed_r[0:half], roll(packed_r[half:QR], 64, 1))
+    fold_l[...] = jnp.where(lane[0:half] < 64, packed_l[0:half], roll(packed_l[half:QR], 64, 1))
     top, bottom = pl.ds(0, 16), pl.ds(H0 - 16, 16)
     body, lo, hi = pl.ds(0, QR), pl.ds(0, 8), pl.ds(QR - 8, 8)
     below, above = pl.ds(QR, 8), pl.ds(QR + 8, 8)
@@ -375,8 +378,10 @@
             (to_left.at[hi], from_r.at[above], 1, -1),
             (to_right.at[lo], from_l.at[below], -1, 1),
             (to_left.at[lo], from_r.at[below], -1, -1),
-            (to_right, from_l.at[body], 0, 1),
-            (to_left, from_r.at[body], 0, -1),
+            (to_right.at[:, pl.ds(0, 128)], from_l.at[body, pl.ds(0, 128)], 0, 1),
+            (to_left.at[:, pl.ds(0, 128)], from_r.at[body, pl.ds(0, 128)], 0, -1),
+            (fold_r, fold_from_l, 0, 1),
+            (fold_l, fold_from_r, 0, -1),
             (raw.at[:, :, bottom], raw.at[:, :, pl.ds(H0 + 16, 16)], 1, 0),
             (raw.at[:, :, top], raw.at[:, :, pl.ds(H0, 16)], -1, 0),
         ])
@@ -449,17 +454,16 @@
     low8 = sub8 < 4
     lane_e = lax.broadcasted_iota(jnp.int32, (ER, 128), 1)
 
-    def from_side(ref, tile):
+    def from_side(ref, folded, tile):
         cols = pl.ds(tile * 128, 128)
-        return jnp.concatenate(
-            [ref[body, cols], jnp.where(low8, ref[below, cols], ref[above, cols])], axis=0
-        )
+        rows = ref[body, cols] if tile == 0 else jnp.concatenate([folded[...], roll(folded[...], 64, 1)], axis=0)
+        return jnp.concatenate([rows, jnp.where(low8, ref[below, cols], ref[above, cols])], axis=0)
 
     for a in range(3):
         pieces = []
         for rp in range(4):
             tile, gi = divmod(a * 4 + rp, 8)
-            side_l, side_r = from_side(from_l, tile), from_side(from_r, tile)
+            side_l, side_r = from_side(from_l, fold_from_l, tile), from_side(from_r, fold_from_r, tile)
             pieces.append(jnp.where(lane_e < 64, roll(side_r, -16 * gi, 1), roll(side_l, 112 - 16 * gi, 1)))
         y = permuted(jnp.concatenate(pieces, axis=0), side[...])
         for rp in range(4):
@@ -570,6 +574,7 @@
             vmem((QR, 256), F32),
             vmem((QR + 16, 256), F32),
             vmem((QR + 16, 256), F32),
+            *([vmem((QR // 2, 128), F32)] * 4),
             phases, phases, phases, phases, phases, phases,
             nine, nine, nine, nine,
             quarter, quarter, quarter, quarter,
@@ -580,8 +585,8 @@
             dma((4, 4)),
             dma((3,)),
             dma((4,)),
-            dma((8,)),
-            dma((8,)),
+            dma((10,)),
+            dma((10,)),
             dma((NR,)),
             dma((NR,)),
             dma((NR,)),

time: 25.5 us -> 25.6 us (level)
  no operation moved by 1% of the time
where the time goes in v6:
time: 25.6 us; the launch traced here: 25.4 us
  Pallas kernels  23.6 us (92%)
  local copies, waits for them, and re-layouts  1.87 us (7%)
    pallas_call x1, Pallas kernels, shards(): pl.pallas_call(kernel, out_shape=jax.ShapeDtypeStruct((H0, W0), F32), in_...  23.6 us
    unnamed x1, local copies, waits for them, and re-layouts  1.87 us

profile of v6, /device:TPU:1, one launch (start us, length us, event | category | flops | bytes accessed | tf_op | source)
XLA Modules:
  0.0 25.4 jit_solution(4830293670075955502)
XLA Ops:
  0.0 23.6 %shard_map.73 = f32[256,512]{1,0:T(8,128)} custom-call(f32[256,512]{1,0:T(8,128)} %lum_h.1, f32[4,256,512]{2,1,0:T(8,128)} %gx_h.1, f32[4,256,512]{2,1,0:T(8,128)} %gy_h.1, s32[256,512]{1,0:T(8,128)} %lab_h.1, bf16[3,544,512]{2,1,0:T(8,128)(2,1)} %constant.6.clone.ct_h, f32[272,512]{1,0:T(8,128)} %constant.7.clone.tab_h, f32[32,8,128]{2,1,0:T(8,128)} %constant.8.clone.dist_h), custom_call_target="tpu_custom_call" | custom-call | tf_op jit(solution)/shard_map/pallas_call | solution.py:557
  23.6 1.9 %copy.9 = f32[256,512]{1,0:T(8,128)} copy(f32[256,512]{1,0:T(8,128)} %shard_map.73) | data formatting | bytes 1048576

commit v7 on v5

--- a/solution.py
+++ b/solution.py
@@ -349,23 +349,6 @@
 
     share_m[r] = in_rows([to_r, to_l, r2, l2])
 
-    pl.semaphore_wait(barrier, len(peers))
-
-    def send(src, dst, send_sem, recv_sem, device):
-        copy = pltpu.make_async_remote_copy(
-            src_ref=src, dst_ref=dst, send_sem=send_sem, recv_sem=recv_sem,
-            device_id=device, device_id_type=MESH,
-        )
-        copy.start()
-        return copy
-
-    copies = [send(share_m.at[r], share_m.at[r], m_send.at[d], m_recv.at[d], (row_peer(d), c)) for d in row_order]
-
-    far = [
-        send(strip.at[r], strip.at[r], r_send.at[i], r_recv.at[i], (row_peer(d), c)) for i, d in enumerate((4, 2, 6))
-    ]
-    near = [send(strip.at[r], strip.at[r], r_send.at[3], r_recv.at[3], (sibling, c))]
-
     lane = lax.broadcasted_iota(jnp.int32, (QR, 128), 1)
     group = lane // 16
     for tile in range(2):
@@ -382,6 +365,23 @@
             packed_l = jnp.where(group == g, roll(edge, 16 * g, 1), packed_l)
         to_right[:, pl.ds(tile * 128, 128)] = packed_r
         to_left[:, pl.ds(tile * 128, 128)] = packed_l
+    pl.semaphore_wait(barrier, len(peers))
+
+    def send(src, dst, send_sem, recv_sem, device):
+        copy = pltpu.make_async_remote_copy(
+            src_ref=src, dst_ref=dst, send_sem=send_sem, recv_sem=recv_sem,
+            device_id=device, device_id_type=MESH,
+        )
+        copy.start()
+        return copy
+
+    copies = [send(share_m.at[r], share_m.at[r], m_send.at[d], m_recv.at[d], (row_peer(d), c)) for d in row_order]
+
+    far = [
+        send(strip.at[r], strip.at[r], r_send.at[i], r_recv.at[i], (row_peer(d), c)) for i, d in enumerate((4, 2, 6))
+    ]
+    near = [send(strip.at[r], strip.at[r], r_send.at[3], r_recv.at[3], (sibling, c))]
+
     top, bottom = pl.ds(0, 16), pl.ds(H0 - 16, 16)
     body, lo, hi = pl.ds(0, QR), pl.ds(0, 8), pl.ds(QR - 8, 8)
     below, above = pl.ds(QR, 8), pl.ds(QR + 8, 8)

time: 25.5 us -> 25.5 us (level)
  no operation moved by 1% of the time
where the time goes in v7:
time: 25.5 us; the launch traced here: 25.3 us
  Pallas kernels  23.4 us (92%)
  local copies, waits for them, and re-layouts  1.87 us (7%)
    pallas_call x1, Pallas kernels, shards(): pl.pallas_call(kernel, out_shape=jax.ShapeDtypeStruct((H0, W0), F32), in_...  23.4 us
    unnamed x1, local copies, waits for them, and re-layouts  1.87 us

profile of v7, /device:TPU:1, one launch (start us, length us, event | category | flops | bytes accessed | tf_op | source)
XLA Modules:
  0.0 25.3 jit_solution(1546886538683218279)
XLA Ops:
  0.0 23.4 %shard_map.73 = f32[256,512]{1,0:T(8,128)} custom-call(f32[256,512]{1,0:T(8,128)} %lum_h.1, f32[4,256,512]{2,1,0:T(8,128)} %gx_h.1, f32[4,256,512]{2,1,0:T(8,128)} %gy_h.1, s32[256,512]{1,0:T(8,128)} %lab_h.1, bf16[3,544,512]{2,1,0:T(8,128)(2,1)} %constant.6.clone.ct_h, f32[272,512]{1,0:T(8,128)} %constant.7.clone.tab_h, f32[32,8,128]{2,1,0:T(8,128)} %constant.8.clone.dist_h), custom_call_target="tpu_custom_call" | custom-call | tf_op jit(solution)/shard_map/pallas_call | solution.py:573
  23.5 1.9 %copy.9 = f32[256,512]{1,0:T(8,128)} copy(f32[256,512]{1,0:T(8,128)} %shard_map.73) | data formatting | bytes 1048576
